TPU v7x, 128 devices: a whole 4x4x4 slice. The times are simulated.
128 devices in a mesh: tm: 8 (over y, core), video: 16 (over x, z).
Axes of the slice: x: 4, y: 4, z: 4, core: 2. Of those that a mesh axis runs over, the one named last changes fastest.
Arguments:
- frame_feats: bfloat16 [128, 128, 32, 768], P('tm', 'video'), may hold values from -192 to 192
- selected: int32 [128, 64], P('tm'), may hold values from 0 to 127, as said below
- counts: int32 [128], P('tm'), may hold values from 8 to 64, as said below
- video_start: int32 [128], replicated, may hold values from 0 to 32736, as said below
- queries: bfloat16 [32, 768], replicated, may hold values from -6 to 6
- frame_pos: bfloat16 [64, 768], replicated, may hold values from -6 to 6
- w_query: bfloat16 [768, 768], replicated, may hold values from -0.21875 to 0.21875
- w_key: bfloat16 [768, 768], replicated, may hold values from -0.21875 to 0.21875
- w_value: bfloat16 [768, 768], replicated, may hold values from -0.21875 to 0.21875
- w_out: bfloat16 [768, 768], replicated, may hold values from -0.21875 to 0.21875
- ln_gain: float32 [768], replicated, may hold values from 0.1 to 1.9
- ln_bias: float32 [768], replicated, may hold values from -3 to 3
- proj_weight: bfloat16 [768, 5120], P(None, 'tm'), may hold values from -0.21875 to 0.21875
- proj_bias: float32 [5120], replicated, may hold values from -3 to 3
- text_embeds: bfloat16 [32768, 5120], P(('tm', 'video')), may hold values from -6 to 6
- norm_gain: float32 [5120], replicated, may hold values from 0.1 to 1.9
Outputs:
- normed: bfloat16 [32768, 5120], P(('tm', 'video'))
Inputs may be any that keep to these rules, and one draw needn't show every extreme that they name: Entry k < counts[w] of video w is a frame of the k-th of counts[w] equal intervals of its 128 frames; later entries are 0. So at most 4 selected frames of one video lie among one device's 8 frames of it, and every draw has a video with 64 selected frames. `counts`: each count is 8 times a power of two; some video has 64 in every draw. `video_start`: the 32 tokens of video w occupy consecutive positions of sequence w // 16 (positions s * 4096 to (s + 1) * 4096 of all, for sequence s), all inside one block of 256 positions k * 256 to (k + 1) * 256 of that sequence; each such block holds the tokens of exactly one video.
All inputs are finite; a program needn't handle non-finite values.
Results may differ from a plain program's by a relative error of at most 0.012.
Values may be sent and summed in bfloat16 or wider, within the bound.
No kernel may reach another device: no remote copies, remote signals or barrier semaphores. Data moves between devices by JAX's collectives and lax.ppermute only.
A program may use at most 128 MiB of HBM per device.

v0:
```python
import math

import jax
import jax.numpy as jnp
from jax import lax
from jax.sharding import PartitionSpec as P

HEADS = 12
HD = 64


def attend(queries, query_vec, key_rows, value_rows, key_live, w_out, ln_gain, ln_bias):
    query_count, width = queries.shape
    head_size = width // HEADS
    scores = jnp.einsum(
        "ihd,nhd->hin",
        query_vec.reshape(query_count, HEADS, head_size),
        key_rows.reshape(-1, HEADS, head_size),
        preferred_element_type=jnp.float32,
    ) * (1.0 / math.sqrt(HD))
    scores = jnp.where(key_live[None, None, :], scores, -jnp.inf)
    row_max = jnp.max(scores, axis=-1, keepdims=True)
    weights_raw = jnp.exp(scores - row_max)
    probabilities = (weights_raw / jnp.sum(weights_raw, axis=-1, keepdims=True)).astype(
        jnp.bfloat16
    )
    context = jnp.einsum(
        "hin,nhd->ihd",
        probabilities,
        value_rows.reshape(-1, HEADS, head_size),
        preferred_element_type=jnp.float32,
    )
    context = context.reshape(query_count, width).astype(jnp.bfloat16)
    residual = jnp.dot(context, w_out, preferred_element_type=jnp.float32) + queries.astype(
        jnp.float32
    )
    row_mean = jnp.mean(residual, axis=-1, keepdims=True)
    variance = jnp.mean(jnp.square(residual - row_mean), axis=-1, keepdims=True)
    return ((residual - row_mean) * lax.rsqrt(variance + 1e-12) * ln_gain + ln_bias).astype(
        jnp.bfloat16
    )


def project_rows(rows, proj_weight, proj_bias):
    return (
        jnp.dot(
            rows,
            lax.all_gather(proj_weight, "tm", axis=1, tiled=True),
            preferred_element_type=jnp.float32,
        )
        + proj_bias
    )


def per_device(
    frame_feats,
    selected,
    counts,
    video_start,
    queries,
    frame_pos,
    w_query,
    w_key,
    w_value,
    w_out,
    ln_gain,
    ln_bias,
    proj_weight,
    proj_bias,
    text_embeds,
    norm_gain,
):
    columns = lax.axis_size("video")
    column = lax.axis_index("video")
    row_index = lax.axis_index("tm")
    frames_here = frame_feats.shape[1]
    tokens_frame = frame_feats.shape[2]
    width = frame_feats.shape[3]
    most = selected.shape[1]
    slots = most // columns
    slot_index = jnp.arange(most, dtype=jnp.int32)
    slot_ids = jnp.arange(slots, dtype=jnp.int32)
    frame_ids = jnp.arange(frames_here, dtype=jnp.int32)
    shifted = selected - column * frames_here
    chosen = (slot_index[None, :] < counts[:, None]) & (shifted >= 0) & (shifted < frames_here)
    pick_rank = jnp.cumsum(chosen.astype(jnp.int32), axis=1) - 1
    pick_table = (
        chosen[:, :, None, None]
        & (pick_rank[:, :, None, None] == slot_ids[None, None, :, None])
        & (shifted[:, :, None, None] == frame_ids[None, None, None, :])
    )
    picker = jnp.any(pick_table, axis=1).astype(jnp.bfloat16)
    outgoing = jnp.einsum(
        "wjf,wfqd->wjqd", picker, frame_feats, preferred_element_type=jnp.float32
    ).astype(jnp.bfloat16)
    my_picks = lax.dynamic_index_in_dim(selected, column, 0, keepdims=False)
    my_count = lax.dynamic_index_in_dim(counts, column, 0, keepdims=False)
    owner_shard = my_picks // frames_here
    valid_slot = slot_index < my_count
    earlier = (
        (slot_index[None, :] < slot_index[:, None])
        & valid_slot[None, :]
        & (owner_shard[None, :] == owner_shard[:, None])
    )
    my_rank = jnp.sum(earlier.astype(jnp.int32), axis=1)
    shard_ids = jnp.arange(columns, dtype=jnp.int32)
    slot_table = (
        valid_slot[None, None, :]
        & (owner_shard[None, None, :] == shard_ids[:, None, None])
        & (my_rank[None, None, :] == slot_ids[None, :, None])
    )
    slot_live = jnp.any(slot_table, axis=2)
    slot_pos = jnp.einsum(
        "sjk,kd->sjd",
        slot_table.astype(jnp.bfloat16),
        frame_pos,
        preferred_element_type=jnp.float32,
    )
    key_input = (
        lax.all_to_all(outgoing, "video", split_axis=0, concat_axis=0, tiled=True).astype(
            jnp.float32
        )
        + slot_pos[:, :, None, :]
    ).astype(jnp.bfloat16)
    key_part = jnp.einsum(
        "sjqd,de->sjqe", key_input, w_key, preferred_element_type=jnp.float32
    ).astype(jnp.bfloat16)
    value_part = jnp.einsum(
        "sjqd,de->sjqe", key_input, w_value, preferred_element_type=jnp.float32
    ).astype(jnp.bfloat16)
    key_rows = key_part
    value_rows = value_part
    key_rows = key_rows.reshape(-1, width)
    value_rows = value_rows.reshape(-1, width)
    key_live = jnp.repeat(slot_live.reshape(-1), tokens_frame)
    query_vec = jnp.dot(queries, w_query, preferred_element_type=jnp.float32).astype(jnp.bfloat16)
    video_out = attend(queries, query_vec, key_rows, value_rows, key_live, w_out, ln_gain, ln_bias)
    length = text_embeds.shape[0]
    query_count = queries.shape[0]
    flat_index = row_index * columns + column
    first_position = flat_index * length
    sequence_starts = lax.dynamic_slice_in_dim(video_start, row_index * columns, columns)
    sequence_videos = jnp.arange(columns, dtype=jnp.int32)
    inside = (sequence_starts >= first_position) & (sequence_starts < first_position + length)
    wanted = jnp.sum(jnp.where(inside, sequence_videos, 0))
    offset = jnp.sum(jnp.where(inside, sequence_starts - first_position, 0))
    sequence_outs = lax.all_gather(video_out, "video", axis=0, tiled=True)
    needed_rows = lax.dynamic_slice_in_dim(sequence_outs, wanted * query_count, query_count)
    projected = project_rows(needed_rows, proj_weight, proj_bias)
    embeds = lax.dynamic_update_slice(
        text_embeds.astype(jnp.float32), projected, (offset, jnp.zeros((), jnp.int32))
    ).astype(jnp.bfloat16)
    wide = embeds.astype(jnp.float32)
    squares = jnp.mean(wide * wide, axis=-1, keepdims=True)
    return (wide * lax.rsqrt(squares + 1e-05) * norm_gain).astype(jnp.bfloat16)


def solution(mesh):
    in_specs = (
        P("tm", "video", None, None),
        P("tm", None),
        P("tm"),
        P(),
        P(),
        P(),
        P(),
        P(),
        P(),
        P(),
        P(),
        P(),
        P(None, "tm"),
        P(),
        P(("tm", "video"), None),
        P(),
    )
    out_specs = P(("tm", "video"), None)
    return jax.shard_map(
        per_device, mesh=mesh, in_specs=in_specs, out_specs=out_specs, check_vma=False
    )
```

profile of v0, /device:TPU:0, one launch (start us, length us, event | category | flops | bytes accessed | tf_op | source)
XLA Modules:
  0.0 170.0 jit_solution(5527464741022111798)
XLA Ops:
  6.5 0.0 copy-start
  6.5 0.0 copy-start.9
  6.5 0.0 copy-start.12
  6.5 0.0 all-gather.2.cloned.1.call-start
  6.5 3.5 %copy.79 = bf16[256,5120]{1,0:T(8,128)(2,1)} copy(bf16[256,5120]{1,0:T(8,128)(2,1)} %param.30) | data formatting | bytes 5242880
  10.0 0.0 all-gather.2.cloned.1.call-update
  10.1 0.0 copy-done.9
  10.1 0.0 copy-done.12
  10.1 0.1 fusion.44
  10.2 0.2 reduce_window_sum.11
  10.4 1.2 and_reduce_fusion
  11.6 6.9 %fusion.5 = bf16[16,4,32,768]{3,1,2,0:T(4,128)(2,1)S(1)} fusion(bf16[16,8,32,768]{3,2,1,0:T(8,128)(2,1)} %param.16, pred[16,4,8]{2,1,0:T(4,128)(4,1)S(1)} %and_reduce_fusion), kind=kOutput, calls=%fused_computation.8 | convolution fusion | flops 25165824 | bytes 9437696 | tf_op jit(solution)/shard_map/wjf,wfqd->wjqd/dot_general | solution.py:93
  18.5 2.4 %copy.76 = bf16[16,4,32,768]{3,2,1,0:T(8,128)(2,1)} copy(bf16[16,4,32,768]{3,1,2,0:T(4,128)(2,1)S(1)} %fusion.5) | data formatting | bytes 6291456 | tf_op jit(solution)/shard_map/wjf,wfqd->wjqd/dot_general | solution.py:93
  20.9 0.0 copy-start.13
  20.9 0.0 copy-start.6
  20.9 0.0 copy-start.3
  20.9 0.0 copy-start.5
  20.9 8.2 %all-to-all-start = ((bf16[16,4,32,768]{3,2,1,0:T(8,128)(2,1)}), bf16[16,4,32,768]{3,2,1,0:T(8,128)(2,1)}, u32[]{:S(2)}, u32[]{:S(2)}) async-start(bf16[16,4,32,768]{3,2,1,0:T(8,128)(2,1)} %copy.76), calls=%async_computation | async-start | bytes 6291456 | tf_op jit(solution)/shard_map/all_to_all | solution.py:120
  29.1 0.0 copy-done.13
  29.1 0.8 select_reduce_fusion
  31.2 0.6 dynamic_slice.14
  31.8 0.6 iota_compare_fusion.6
  32.5 0.2 convert_reduce_fusion
  32.7 0.0 copy-done.6
  32.7 0.2 fusion.27
  32.8 0.1 copy.52
  33.0 0.2 and_reduce_fusion.1
  33.1 0.1 copy.53
  33.2 0.1 reshape.191
  33.3 0.1 broadcast_in_dim.16
  33.4 0.1 broadcast_in_dim.17
  33.5 0.0 copy-done.3
  33.5 0.0 copy-done.5
  33.5 0.3 convolution_convert_fusion
  33.8 0.1 reshape.192
  35.3 36.3 %all-to-all-done = bf16[16,4,32,768]{3,2,1,0:T(8,128)(2,1)} async-done(((bf16[16,4,32,768]{3,2,1,0:T(8,128)(2,1)}), bf16[16,4,32,768]{3,2,1,0:T(8,128)(2,1)}, u32[]{:S(2)}, u32[]{:S(2)}) %all-to-all-start) | async-done | bytes 3145760 | tf_op jit(solution)/shard_map/all_to_all | solution.py:120
  71.6 0.0 copy-done
  71.6 6.3 %fusion.17 = bf16[16,4,32,768]{3,2,1,0:T(8,128)(2,1)} fusion(bf16[16,4,32,768]{3,2,1,0:T(8,128)(2,1)} %all-to-all-done, f32[16,4,768]{2,1,0:T(4,128)S(1)} %copy.52, bf16[768,768]{1,0:T(8,128)(2,1)S(1)} %copy-done), kind=kOutput, calls=%fused_computation.22 | convolution fusion | flops 2422210560 | bytes 7667712 | tf_op jit(solution)/shard_map/sjqd,de->sjqe/dot_general | solution.py:125
  77.9 10.6 %reshape_reshape.7 = bf16[2048,12,64]{2,1,0:T(8,128)(2,1)} reshape(bf16[16,4,32,768]{3,2,1,0:T(8,128)(2,1)} %fusion.17) | data formatting | bytes 6291456 | tf_op jit(solution)/shard_map/reshape;reshape | solution.py:18
  88.5 6.6 %fusion.16 = bf16[16,4,32,768]{3,2,1,0:T(8,128)(2,1)} fusion(bf16[16,4,32,768]{3,2,1,0:T(8,128)(2,1)} %all-to-all-done, f32[16,4,768]{2,1,0:T(4,128)S(1)} %copy.52, bf16[768,768]{1,0:T(8,128)(2,1)} %param.24), kind=kOutput, calls=%fused_computation.21 | convolution fusion | flops 2422210560 | bytes 7667712 | tf_op jit(solution)/shard_map/sjqd,de->sjqe/dot_general | solution.py:128
  95.0 10.6 %reshape_reshape.6 = bf16[2048,12,64]{2,1,0:T(8,128)(2,1)} reshape(bf16[16,4,32,768]{3,2,1,0:T(8,128)(2,1)} %fusion.16) | data formatting | bytes 6291456 | tf_op jit(solution)/shard_map/reshape;reshape | solution.py:30
  105.6 7.0 %multiply_select_fusion = f32[12,32,2048]{2,1,0:T(8,128)S(1)} fusion(bf16[2048,12,64]{2,1,0:T(8,128)(2,1)} %reshape_reshape.7, pred[2048]{0:T(1024)(128)(4,1)S(1)} %broadcast_in_dim.17, bf16[32,12,64]{2,1,0:T(8,128)(2,1)S(1)} %reshape.192), kind=kOutput, calls=%fused_computation.17 | convolution fusion | flops 102236160 | bytes 6342656 | tf_op jit(solution)/shard_map/ihd,nhd->hin/dot_general | solution.py:15
  112.6 0.0 copy-start.2
  112.6 1.7 copy-done.2
  114.3 0.6 fusion.46
  114.9 0.0 copy-start.7
  114.9 9.0 %fusion.24 = bf16[32,12,64]{2,0,1:T(8,128)(2,1)S(1)} fusion(bf16[2048,12,64]{2,1,0:T(8,128)(2,1)} %reshape_reshape.6, f32[12,32]{1,0:T(8,128)S(1)} %fusion.46, f32[12,32,2048]{2,1,0:T(8,128)} %copy-done.2), kind=kOutput, calls=%fused_computation.27 | convolution fusion | flops 103049600 | bytes 6342144 | tf_op jit(solution)/shard_map/hin,nhd->ihd/dot_general | solution.py:27
  124.0 0.1 convert_element_type.68
  124.1 0.0 copy-done.4
  124.1 0.4 fusion.47
  124.6 0.2 multiply_reduce_fusion
  124.8 0.0 copy-done.10
  124.8 0.0 copy-done.11
  124.8 0.1 add_convert_fusion.7
  124.9 25.8 %all_gather.6 = bf16[512,768]{1,0:T(8,128)(2,1)S(1)} all-gather(bf16[32,768]{1,0:T(8,128)(2,1)S(1)} %add_convert_fusion.7), channel_id=1, replica_groups=mesh['tm'=8,'video'=16] {'video'}, dimensions={0}, use_global_device_ids=true | all-gather | bytes 835584 | tf_op jit(solution)/shard_map/all_gather | solution.py:147
  150.7 0.0 all-gather.2.cloned.1.call-done
  150.7 0.0 copy-done.7
  150.7 4.7 %convolution_add_fusion = bf16[32,5120]{1,0:T(8,128)(2,1)S(1)} fusion(bf16[768,5120]{1,0:T(8,128)(2,1)} %all-gather.2.cloned.1.call-done, f32[5120]{0:T(1024)S(1)} %copy-done.7, bf16[512,768]{1,0:T(8,128)(2,1)S(1)} %all_gather.6, s32[]{:T(128)S(6)} %select_n.48), kind=kOutput, calls=%fused_computation.11 | convolution fusion | flops 251985920 | bytes 8261636 | tf_op jit(solution)/shard_map/dot_general | solution.py:46
  155.4 0.0 copy-start.8
  155.5 2.9 %dynamic_update_slice.3 = bf16[256,5120]{1,0:T(8,128)(2,1)} dynamic-update-slice(bf16[256,5120]{1,0:T(8,128)(2,1)} %copy.79, bf16[32,5120]{1,0:T(8,128)(2,1)S(1)} %convolution_add_fusion, s32[]{:T(128)S(6)} %select_n.50, s32[]{:T(128)} %constant.24.clone.1) | dynamic-update-slice | bytes 655364 | tf_op jit(solution)/shard_map/dynamic_update_slice | solution.py:150
  158.3 2.5 %fusion.7 = f32[256]{0:T(256)S(1)} fusion(bf16[256,5120]{1,0:T(8,128)(2,1)} %dynamic_update_slice.3), kind=kLoop, calls=%fused_computation.12 | loop fusion | flops 3931904 | bytes 2622464 | tf_op jit(solution)/shard_map/reduce_sum | solution.py:154
  160.8 0.0 copy-done.8
  160.9 0.0 copy-done.1
  160.9 2.3 %fusion.9 = bf16[256,5120]{1,0:T(8,128)(2,1)} fusion(f32[5120]{0:T(1024)S(1)} %copy-done.8, f32[256]{0:T(256)S(1)} %add_rsqrt_fusion, bf16[256,5120]{1,0:T(8,128)(2,1)S(1)} %copy-done.1), kind=kLoop, calls=%fused_computation.14 | loop fusion | flops 5242880 | bytes 5264384 | tf_op jit(solution)/shard_map/convert_element_type | solution.py:155
  (15 shorter events, 0.2 us)
Async XLA Ops:
  6.5 65.1 %copy-start = (bf16[768,768]{1,0:T(8,128)(2,1)S(1)}, bf16[768,768]{1,0:T(8,128)(2,1)}, u32[]{:S(2)}) copy-start(bf16[768,768]{1,0:T(8,128)(2,1)} %param.23) | copy-start | bytes 3538948
  6.5 3.5 %copy-start.9 = (s32[16,64]{1,0:T(8,128)S(1)}, s32[16,64]{1,0:T(8,128)}, u32[]{:S(2)}) copy-start(s32[16,64]{1,0:T(8,128)} %param.17) | copy-start | bytes 12292
  6.5 3.5 %copy-start.12 = (s32[16]{0:T(128)S(1)}, s32[16]{0:T(128)}, u32[]{:S(2)}) copy-start(s32[16]{0:T(128)} %param.18) | copy-start | bytes 196
  6.5 144.2 %all-gather.2.cloned.1.call-start = ((), (), s32[]{:S(2)}) async-start(), calls=%async_computation.1 | async-start | bytes 8847360 | tf_op jit(solution)/shard_map/all_gather | solution.py:48
  20.9 8.2 %copy-start.13 = (s32[128]{0:T(128)S(1)}, s32[128]{0:T(128)}, u32[]{:S(2)}) copy-start(s32[128]{0:T(128)} %param.19) | copy-start | bytes 1540
  20.9 11.7 %copy-start.6 = (bf16[64,768]{1,0:T(8,128)(2,1)S(1)}, bf16[64,768]{1,0:T(8,128)(2,1)}, u32[]{:S(2)}) copy-start(bf16[64,768]{1,0:T(8,128)(2,1)} %param.21) | copy-start | bytes 294916
  20.9 12.6 %copy-start.3 = (bf16[768,768]{1,0:T(8,128)(2,1)S(1)}, bf16[768,768]{1,0:T(8,128)(2,1)}, u32[]{:S(2)}) copy-start(bf16[768,768]{1,0:T(8,128)(2,1)} %param.22) | copy-start | bytes 3538948
  20.9 12.6 %copy-start.5 = (bf16[32,768]{1,0:T(8,128)(2,1)S(1)}, bf16[32,768]{1,0:T(8,128)(2,1)}, u32[]{:S(2)}) copy-start(bf16[32,768]{1,0:T(8,128)(2,1)} %param.20) | copy-start | bytes 147460
  20.9 50.7 %all-to-all-start = ((bf16[16,4,32,768]{3,2,1,0:T(8,128)(2,1)}), bf16[16,4,32,768]{3,2,1,0:T(8,128)(2,1)}, u32[]{:S(2)}, u32[]{:S(2)}) async-start(bf16[16,4,32,768]{3,2,1,0:T(8,128)(2,1)} %copy.76), calls=%async_computation | async-start | bytes 6291456 | tf_op jit(solution)/shard_map/all_to_all | solution.py:120
  112.6 1.7 copy-start.2
  114.9 9.2 %copy-start.4 = (bf16[768,768]{1,0:T(8,128)(2,1)S(1)}, bf16[768,768]{1,0:T(8,128)(2,1)}, u32[]{:S(2)}) copy-start(bf16[768,768]{1,0:T(8,128)(2,1)} %param.25) | copy-start | bytes 3538948
  114.9 9.9 %copy-start.10 = (f32[768]{0:T(1024)S(1)}, f32[768]{0:T(1024)}, u32[]{:S(2)}) copy-start(f32[768]{0:T(1024)} %param.27) | copy-start | bytes 9220
  114.9 9.9 %copy-start.11 = (f32[768]{0:T(1024)S(1)}, f32[768]{0:T(1024)}, u32[]{:S(2)}) copy-start(f32[768]{0:T(1024)} %param.26) | copy-start | bytes 9220
  114.9 35.8 %copy-start.7 = (f32[5120]{0:T(1024)S(1)}, f32[5120]{0:T(1024)}, u32[]{:S(2)}) copy-start(f32[5120]{0:T(1024)} %param.29) | copy-start | bytes 61444
  155.4 5.4 %copy-start.8 = (f32[5120]{0:T(1024)S(1)}, f32[5120]{0:T(1024)}, u32[]{:S(2)}) copy-start(f32[5120]{0:T(1024)} %param.31) | copy-start | bytes 61444
  158.3 2.5 %copy-start.1 = (bf16[256,5120]{1,0:T(8,128)(2,1)S(1)}, bf16[256,5120]{1,0:T(8,128)(2,1)}, u32[]{:S(2)}) copy-start(bf16[256,5120]{1,0:T(8,128)(2,1)} %dynamic_update_slice.3) | copy-start | bytes 7864324
Sparse Core Ops, SparseCore 0:
  10.2 49.9 all-gather.1
where the time goes:
time: 171 us; the launch traced here: 170 us
  matrix products  41.3 us (24%)
  waiting for transfers between devices  36.3 us (21%)
  local copies, waits for them, and re-layouts  33.1 us (19%)
  blocking collectives  25.8 us (15%)
  between operations  16.3 us (10%)
  other arithmetic  9 us (5%)
  starting transfers between devices  8.16 us (5%)
    all_to_all x1, waiting for transfers between devices, per_device(): lax.all_to_all(outgoing, 'video', split_axis=0, concat_axis=0, tiled=True)  36.3 us
    all_gather x1, blocking collectives, per_device(): sequence_outs = lax.all_gather(video_out, 'video', axis=0, tiled=True)  25.8 us
    another operation x1, local copies, waits for them, and re-layouts, attend(): value_rows.reshape(-1, HEADS, head_size)  10.6 us
    another operation x1, local copies, waits for them, and re-layouts, attend(): key_rows.reshape(-1, HEADS, head_size)  10.6 us
    dot_general x1, matrix products, attend(): jnp.einsum('hin,nhd->ihd', probabilities, value_rows.reshape(-1, HEADS, h...  9 us
    all_to_all x1, starting transfers between devices, per_device(): lax.all_to_all(outgoing, 'video', split_axis=0, concat_axis=0, tiled=True)  8.16 us
    dot_general x1, matrix products, attend(): jnp.einsum('ihd,nhd->hin', query_vec.reshape(query_count, HEADS, head_siz...  6.98 us
    dot_general x1, matrix products, per_device(): jnp.einsum('wjf,wfqd->wjqd', picker, frame_feats, preferred_element_type=...  6.9 us
  transfers between devices with their start and end apart: 2, of which 1 were waited for; matrix products, arithmetic and copies ran while one was open for 39% of the time, Pallas kernels for 0%

commit v1 on v0

v1 whole, which is shorter than its diff:
```python
import math

import jax
import jax.numpy as jnp
from jax import lax
from jax.experimental import pallas as pl
from jax.experimental.pallas import tpu as pltpu
from jax.sharding import PartitionSpec as P

HEADS = 12
HD = 64
WIDTH = HEADS * HD
VQ = 32
QF = 32
DL = 5120
SLOTS = 4
COLUMNS = 16
BLOCK = 256
WINDOW = 48
STATS = 128
CHUNK = 4
GROUP = 4
NEG = -1e30
MIB = 1 << 20

f32 = jnp.float32
bf16 = jnp.bfloat16


def iota(shape, axis):
    return lax.broadcasted_iota(jnp.int32, shape, axis)


def attend_kernel(
    selected_in, counts_in, starts_in, frames, pos_in, queries_in, w_query_in, w_key_in, w_value_in, out,
    selected, counts, starts, pos, queries, w_query, w_key, w_value, x_raw, x_keys, folded, pos_wide,
    scalar_sems, sems, weight_sems,
):
    row = lax.axis_index("tm")
    column = lax.axis_index("video")
    scalars = [
        pltpu.make_async_copy(source, target, scalar_sems.at[i])
        for i, (source, target) in enumerate(
            ((selected_in, selected), (counts_in, counts), (starts_in, starts))
        )
    ]
    loads = [
        pltpu.make_async_copy(source, target, weight_sems.at[i])
        for i, (source, target) in enumerate((
            (queries_in, queries), (w_query_in, w_query), (w_key_in, w_key), (pos_in, pos),
            (w_value_in, w_value),
        ))
    ]
    for copy in scalars + loads:
        copy.start()
    for copy in scalars:
        copy.wait()

    def slot(video, j):
        count = counts[video]
        last = jnp.maximum(count >> 4, 1) - 1
        k = ((column * count) >> 4) + jnp.minimum(j, last)
        frame = selected[video, k] - column * 8
        live = (j <= last) & (frame >= 0) & (frame < 8)
        return k, jnp.clip(frame, 0, 7), live

    @pl.loop(0, COLUMNS)
    def _(video):
        for j in range(SLOTS):
            _, frame, _ = slot(video, j)
            pltpu.make_async_copy(
                frames.at[video, frame], x_raw.at[video * SLOTS + j], sems.at[video]
            ).start()

    for copy in loads[:3]:
        copy.wait()
    query = jnp.dot(queries[...], w_query[...], preferred_element_type=f32).astype(bf16)
    query = query * jnp.asarray(1.0 / math.sqrt(HD), bf16)
    for g in range(HEADS // GROUP):
        wide = GROUP * HD
        part = query[:, g * wide:(g + 1) * wide]
        part = jnp.concatenate([part] * GROUP, axis=0)
        same = iota(part.shape, 0) // VQ == iota(part.shape, 1) // HD
        part = jnp.where(same, part, jnp.zeros_like(part))
        fold = lax.dot_general(
            part, w_key[:, g * wide:(g + 1) * wide], (((1,), (1,)), ((), ())),
            preferred_element_type=f32,
        )
        high = fold.astype(bf16)
        rows = GROUP * VQ
        folded[g * rows:(g + 1) * rows, :] = high
        folded[HEADS * VQ + g * rows:HEADS * VQ + (g + 1) * rows, :] = (
            fold - high.astype(f32)
        ).astype(bf16)
    for copy in loads[3:]:
        copy.wait()
    pos_wide[...] = pos[...].astype(f32)

    lane = iota((VQ, STATS), 1)
    stat_head = lane % HEADS
    stat_part = lane // HEADS
    piece = stat_part % 3

    @pl.loop(0, COLUMNS // CHUNK)
    def _(chunk):
        lives = []
        for t in range(CHUNK):
            video = chunk * CHUNK + t
            pltpu.make_async_copy(
                frames.at[video, pl.ds(0, SLOTS)], x_raw.at[pl.ds(video * SLOTS, SLOTS)], sems.at[video]
            ).wait()
            alive = jnp.int32(0)
            for j in range(SLOTS):
                k, _, live = slot(video, j)
                alive = alive + live.astype(jnp.int32)
                x = x_raw[video * SLOTS + j].astype(f32) + pos_wide[pl.ds(k, 1), :]
                at = (t * SLOTS + j) * QF
                x_keys[at:at + QF, :] = x.astype(bf16)
            lives.append(alive)
        x = x_keys[...]
        both = lax.dot_general(folded[...], x, (((1,), (1,)), ((), ())), preferred_element_type=f32)
        scores = both[:HEADS * VQ] + both[HEADS * VQ:]
        values = jnp.dot(x, w_value[...], preferred_element_type=f32).astype(bf16)
        keys = SLOTS * QF
        for t in range(CHUNK):
            video = chunk * CHUNK + t
            hidden = jnp.where(iota((1, keys), 1) < lives[t] * QF, 0.0, NEG)
            s = scores[:, t * keys:(t + 1) * keys] + hidden
            top = jnp.max(s, axis=1, keepdims=True)
            p = jnp.exp(s - top)
            total = jnp.sum(p, axis=1, keepdims=True)
            p = p.astype(bf16)
            block = ((starts[row * COLUMNS + video] - row * (COLUMNS * BLOCK)) >> 8) & (COLUMNS - 1)
            for g in range(HEADS // GROUP):
                wide = GROUP * HD
                rows = GROUP * VQ
                full = jnp.dot(
                    p[g * rows:(g + 1) * rows], values[t * keys:(t + 1) * keys, g * wide:(g + 1) * wide],
                    preferred_element_type=f32,
                )
                head = iota((VQ, wide), 1) // HD
                context = full[:VQ]
                for h in range(1, GROUP):
                    context = jnp.where(head == h, full[h * VQ:(h + 1) * VQ], context)
                out[block, :, g * wide:(g + 1) * wide] = context.astype(bf16)
            stat = jnp.zeros((VQ, STATS), f32)
            for h in range(HEADS):
                one = jnp.where(stat_part < 3, top[h * VQ:(h + 1) * VQ], total[h * VQ:(h + 1) * VQ])
                stat = jnp.where(stat_head == h, one, stat)
            high = stat.astype(bf16).astype(f32)
            mid = (stat - high).astype(bf16).astype(f32)
            low = stat - high - mid
            stat = jnp.where(piece == 0, high, jnp.where(piece == 1, mid, low))
            stat = jnp.where(stat_part < 6, stat, 0.0)
            out[block, :, WIDTH:] = stat.astype(bf16)


def attend(selected, counts, starts, frames, pos, queries, w_query, w_key, w_value):
    return pl.pallas_call(
        attend_kernel,
        out_shape=jax.ShapeDtypeStruct((COLUMNS, VQ, WIDTH + STATS), bf16),
        in_specs=[pl.BlockSpec(memory_space=pl.ANY)] * 9,
        out_specs=pl.BlockSpec(memory_space=pltpu.VMEM),
        scratch_shapes=[
            pltpu.SMEM(selected.shape, jnp.int32),
            pltpu.SMEM(counts.shape, jnp.int32),
            pltpu.SMEM(starts.shape, jnp.int32),
            pltpu.VMEM(pos.shape, bf16),
            pltpu.VMEM(queries.shape, bf16),
            pltpu.VMEM((WIDTH, WIDTH), bf16),
            pltpu.VMEM((WIDTH, WIDTH), bf16),
            pltpu.VMEM((WIDTH, WIDTH), bf16),
            pltpu.VMEM((COLUMNS * SLOTS, QF, WIDTH), bf16),
            pltpu.VMEM((CHUNK * SLOTS * QF, WIDTH), bf16),
            pltpu.VMEM((2 * HEADS * VQ, WIDTH), bf16),
            pltpu.VMEM(pos.shape, f32),
            pltpu.SemaphoreType.DMA((3,)),
            pltpu.SemaphoreType.DMA((COLUMNS,)),
            pltpu.SemaphoreType.DMA((5,)),
        ],
        compiler_params=pltpu.CompilerParams(vmem_limit_bytes=60 * MIB),
        cost_estimate=pl.CostEstimate(
            flops=9_000_000_000, bytes_accessed=8_000_000, transcendentals=800_000
        ),
        name="attend",
    )(selected, counts, starts, frames, pos, queries, w_query, w_key, w_value)


def combine_kernel(parts, queries, w_out, gain, bias, out):
    stat = parts[:, :, WIDTH:].astype(f32).reshape(COLUMNS * VQ, STATS)

    def shifted(n):
        return pltpu.roll(stat, STATS - n * HEADS, 1)

    tops = stat + shifted(1) + shifted(2)
    totals = shifted(3) + shifted(4) + shifted(5)
    lane = iota((VQ, STATS), 1)
    real = lane < HEADS
    tops = [jnp.where(real, tops[c * VQ:(c + 1) * VQ], 0.0) for c in range(COLUMNS)]
    totals = [jnp.where(real, totals[c * VQ:(c + 1) * VQ], 1.0) for c in range(COLUMNS)]
    top = tops[0]
    for c in range(1, COLUMNS):
        top = jnp.maximum(top, tops[c])
    scales = [jnp.exp(t - top) for t in tops]
    total = scales[0] * totals[0]
    for c in range(1, COLUMNS):
        total = total + scales[c] * totals[c]
    inverse = jnp.where(real, 1.0 / total, 0.0)
    weight = jnp.concatenate([s * inverse for s in scales], axis=0)
    high = weight.astype(bf16)
    low = (weight - high.astype(f32)).astype(bf16)
    spread = (iota((2 * STATS, WIDTH), 0) % STATS == iota((2 * STATS, WIDTH), 1) // HD).astype(f32).astype(bf16)
    weight = jnp.dot(jnp.concatenate([high, low], axis=1), spread, preferred_element_type=f32)
    context = jnp.zeros((VQ, WIDTH), f32)
    for c in range(COLUMNS):
        context = context + weight[c * VQ:(c + 1) * VQ] * parts[c, :, :WIDTH].astype(f32)
    residual = jnp.dot(context.astype(bf16), w_out[...], preferred_element_type=f32) + queries[...].astype(f32)
    mean = jnp.mean(residual, axis=-1, keepdims=True)
    centred = residual - mean
    variance = jnp.mean(centred * centred, axis=-1, keepdims=True)
    out[...] = (centred * lax.rsqrt(variance + 1e-12) * gain[...] + bias[...]).astype(bf16)


def combine(parts, queries, w_out, gain, bias):
    vmem = pl.BlockSpec(memory_space=pltpu.VMEM)
    return pl.pallas_call(
        combine_kernel,
        out_shape=jax.ShapeDtypeStruct((VQ, WIDTH), bf16),
        in_specs=[vmem] * 5,
        out_specs=vmem,
        compiler_params=pltpu.CompilerParams(vmem_limit_bytes=24 * MIB),
        name="combine",
    )(parts, queries, w_out, gain.reshape(1, WIDTH), bias.reshape(1, WIDTH))


def project_kernel(rows, w0, w1, w2, w3, bias, out):
    here = lax.axis_index("tm")
    half = here // 4
    wide = w0.shape[1]
    for j, w in enumerate((w0, w1, w2, w3)):
        at = pl.multiple_of(((here % 4) ^ j) * wide, 128)
        shift = pl.multiple_of(half * (4 * wide) + at, 128)
        result = jnp.dot(rows[...], w[...], preferred_element_type=f32) + bias[:, pl.ds(shift, wide)]
        out[:, pl.ds(at, wide)] = result.astype(bf16)


def project(rows, weights, bias):
    vmem = pl.BlockSpec(memory_space=pltpu.VMEM)
    return pl.pallas_call(
        project_kernel,
        out_shape=jax.ShapeDtypeStruct((VQ, DL // 2), bf16),
        in_specs=[vmem] * 6,
        out_specs=vmem,
        compiler_params=pltpu.CompilerParams(vmem_limit_bytes=24 * MIB),
        cost_estimate=pl.CostEstimate(flops=126_000_000, bytes_accessed=4_200_000, transcendentals=0),
        name="project",
    )(rows, *weights, bias)


def norm_rows(wide, gain):
    squares = jnp.mean(wide * wide, axis=-1, keepdims=True)
    return (wide * lax.rsqrt(squares + 1e-05) * gain).astype(bf16)


def text_kernel(text, gain, out):
    out[...] = norm_rows(text[...].astype(f32), gain[...])


def norm_text(text, gain):
    rows = 64
    return pl.pallas_call(
        text_kernel,
        out_shape=jax.ShapeDtypeStruct(text.shape, bf16),
        grid=(text.shape[0] // rows,),
        in_specs=[
            pl.BlockSpec((rows, DL), lambda i: (i, 0)),
            pl.BlockSpec((1, DL), lambda i: (0, 0)),
        ],
        out_specs=pl.BlockSpec((rows, DL), lambda i: (i, 0)),
        compiler_params=pltpu.CompilerParams(vmem_limit_bytes=24 * MIB),
        cost_estimate=pl.CostEstimate(flops=8_000_000, bytes_accessed=5_300_000, transcendentals=256),
        name="norm_text",
    )(text, gain)


def place_kernel(starts, mine, other, gain, text, normed, out, text_rows, embeds, done_rows, sems):
    row = lax.axis_index("tm")
    column = lax.axis_index("video")
    first = (row * COLUMNS + column) * BLOCK
    offset = jnp.int32(0)
    for w in range(COLUMNS):
        at = starts[row * COLUMNS + w] - first
        offset = offset + jnp.where((at >= 0) & (at < BLOCK), at, 0)
    begin = pl.multiple_of(jnp.minimum(offset >> 4, (BLOCK - WINDOW) // 16) * 16, 16)
    fetch = pltpu.make_async_copy(text.at[pl.ds(begin, WINDOW)], text_rows, sems.at[0])
    fetch.start()
    shift = offset - begin
    pick = (iota((WINDOW, VQ), 0) - shift == iota((WINDOW, VQ), 1)).astype(f32).astype(bf16)
    half = row // 4
    wide = DL // 2
    embeds[:, pl.ds(pl.multiple_of(half * wide, 128), wide)] = jnp.dot(
        pick, mine[...], preferred_element_type=f32
    )
    embeds[:, pl.ds(pl.multiple_of((1 - half) * wide, 128), wide)] = jnp.dot(
        pick, other[...], preferred_element_type=f32
    )
    place = iota((WINDOW, DL), 0) - shift
    fetch.wait()
    rows = jnp.where((place >= 0) & (place < VQ), embeds[...], text_rows[...].astype(f32))
    done_rows[...] = norm_rows(rows, gain[...])
    store = pltpu.make_async_copy(done_rows, out.at[pl.ds(begin, WINDOW)], sems.at[1])
    store.start()
    store.wait()


def place(starts, mine, other, gain, text, normed):
    vmem = pl.BlockSpec(memory_space=pltpu.VMEM)
    anywhere = pl.BlockSpec(memory_space=pl.ANY)
    return pl.pallas_call(
        place_kernel,
        out_shape=jax.ShapeDtypeStruct(normed.shape, bf16),
        in_specs=[pl.BlockSpec(memory_space=pltpu.SMEM), vmem, vmem, vmem, anywhere, anywhere],
        out_specs=anywhere,
        input_output_aliases={5: 0},
        scratch_shapes=[
            pltpu.VMEM((WINDOW, DL), bf16),
            pltpu.VMEM((WINDOW, DL), f32),
            pltpu.VMEM((WINDOW, DL), bf16),
            pltpu.SemaphoreType.DMA((2,)),
        ],
        compiler_params=pltpu.CompilerParams(vmem_limit_bytes=24 * MIB),
        name="place",
    )(starts, mine, other, gain, text, normed)


def per_device(
    frame_feats, selected, counts, video_start, queries, frame_pos, w_query, w_key, w_value, w_out,
    ln_gain, ln_bias, proj_weight, proj_bias, text_embeds, norm_gain,
):
    def swap(x, mask):
        return lax.ppermute(x, "tm", [(k, k ^ mask) for k in range(8)])

    near = swap(proj_weight, 2)
    twin = swap(proj_weight, 1)
    parts = attend(
        selected, counts, video_start, frame_feats, frame_pos, queries, w_query, w_key, w_value
    )
    gain = norm_gain.reshape(1, DL)
    parts, text = lax.optimization_barrier((parts, text_embeds))
    received = lax.all_to_all(parts, "video", split_axis=0, concat_axis=0, tiled=True)
    normed = norm_text(text, gain)
    received, normed, near = lax.optimization_barrier((received, normed, near))
    rows = combine(received, queries, w_out, ln_gain, ln_bias)
    weights = (proj_weight, twin, near, swap(near, 1))
    bias = proj_bias.reshape(1, DL)
    other_rows = swap(rows, 6)
    mine = project(rows, weights, bias)
    other_rows, mine = lax.optimization_barrier((other_rows, mine))
    theirs = project(other_rows, weights, bias)
    other = swap(theirs, 6)
    return place(video_start, mine, other, gain, text_embeds, normed)


def solution(mesh):
    in_specs = (
        P("tm", "video", None, None), P("tm", None), P("tm"), P(), P(), P(), P(), P(), P(), P(),
        P(), P(), P(None, "tm"), P(), P(("tm", "video"), None), P(),
    )
    return jax.shard_map(
        per_device, mesh=mesh, in_specs=in_specs, out_specs=P(("tm", "video"), None), check_vma=False
    )
```

time: 171 us -> 58.6 us (0.34)
  the two profiles are of different devices: /device:TPU:0 before, /device:TPU:1 now
where the time goes in v1:
time: 58.6 us; the launch traced here: 58.2 us
  Pallas kernels  22.8 us (39%)
  starting transfers between devices  17.1 us (29%)
  waiting for transfers between devices  14.6 us (25%)
  local copies, waits for them, and re-layouts  3.55 us (6%)
    pallas_call x1, Pallas kernels, attend(): pl.pallas_call(attend_kernel, out_shape=jax.ShapeDtypeStruct((COLUMNS, VQ...  12.3 us
    ppermute x5, starting transfers between devices, swap(): return lax.ppermute(x, 'tm', [(k, k ^ mask) for k in range(8)])  9.69 us
    all_to_all x1, waiting for transfers between devices, per_device(): lax.all_to_all(parts, 'video', split_axis=0, concat_axis=0, tiled=True)  9.12 us
    all_to_all x1, starting transfers between devices, per_device(): lax.all_to_all(parts, 'video', split_axis=0, concat_axis=0, tiled=True)  7.44 us
    ppermute x5, waiting for transfers between devices, swap(): return lax.ppermute(x, 'tm', [(k, k ^ mask) for k in range(8)])  5.49 us
    pallas_call x2, Pallas kernels, project(): pl.pallas_call(project_kernel, out_shape=jax.ShapeDtypeStruct((VQ, DL //...  4.42 us
    unnamed x22, local copies, waits for them, and re-layouts  3.54 us
    pallas_call x1, Pallas kernels, norm_text(): pl.pallas_call(text_kernel, out_shape=jax.ShapeDtypeStruct(text.shape, bf...  2.8 us
  transfers between devices with their start and end apart: 6, of which 2 were waited for; matrix products, arithmetic and copies ran while one was open for 0% of the time, Pallas kernels for 32%

profile of v1, /device:TPU:1, one launch (start us, length us, event | category | flops | bytes accessed | tf_op | source)
XLA Modules:
  0.0 58.2 jit_solution(8258738792716369775)
XLA Ops:
  0.0 2.1 %collective-permute-start = (bf16[768,640]{1,0:T(8,128)(2,1)}, bf16[768,640]{1,0:T(8,128)(2,1)}, u32[]{:S(2)}, u32[]{:S(2)}) collective-permute-start(bf16[768,640]{1,0:T(8,128)(2,1)} %w0.3), channel_id=1, source_target_pairs={{0,32},{16,48},{32,0},{48,16},{64,96},{80,112},{96,64},{112,80},{1... | collective-permute-start | bytes 2949128 | tf_op jit(solution)/shard_map/ppermute | solution.py:341
  2.1 0.0 copy-start
  2.1 12.3 %attend.1 = bf16[16,32,896]{2,1,0:T(8,128)(2,1)} custom-call(s32[16,64]{1,0:T(8,128)} %selected_in.1, s32[16]{0:T(128)} %counts_in.1, s32[128]{0:T(128)} %starts.1, bf16[16,8,32,768]{3,2,1,0:T(8,128)(2,1)} %frames.1, bf16[64,768]{1,0:T(8,128)(2,1)} %pos_in.1, bf16[32,768]{1,0:T(8,128)(2,1)} %queries.1, bf16[768,768]{1,0:T(8,128)(2,1)} %w_query_in.1, ...), custom_call_target="tpu_custom_call" | custom-call | flops 8999999488 | bytes 8000000 | tf_op jit(solution)/shard_map/attend/pallas_call | solution.py:159
  14.4 7.4 %all-to-all-start = ((bf16[16,32,896]{2,1,0:T(8,128)(2,1)}), bf16[16,32,896]{2,1,0:T(8,128)(2,1)S(1)}, u32[]{:S(2)}, u32[]{:S(2)}) async-start(bf16[16,32,896]{2,1,0:T(8,128)(2,1)} %attend.1), calls=%async_computation | async-start | bytes 1835008 | tf_op jit(solution)/shard_map/all_to_all | solution.py:350
  21.9 1.3 %collective-permute-start.2 = (bf16[768,640]{1,0:T(8,128)(2,1)}, bf16[768,640]{1,0:T(8,128)(2,1)}, u32[]{:S(2)}, u32[]{:S(2)}) collective-permute-start(bf16[768,640]{1,0:T(8,128)(2,1)} %w0.3), channel_id=1, source_target_pairs={{0,16},{16,0},{32,48},{48,32},{64,80},{80,64},{96,112},{112,96},{1... | collective-permute-start | bytes 2949128 | tf_op jit(solution)/shard_map/ppermute | solution.py:341
  23.2 0.0 copy-done
  23.2 0.0 copy-start.5
  23.2 0.7 %copy-done.5 = f32[5120]{0:T(1024)S(1)} copy-done((f32[5120]{0:T(1024)S(1)}, f32[5120]{0:T(1024)}, u32[]{:S(2)}) %copy-start.5) | copy-done | bytes 20504
  23.9 0.0 copy-start.9
  23.9 0.0 copy-start.10
  23.9 2.8 %norm_text.1.normed = bf16[256,5120]{1,0:T(8,128)(2,1)} custom-call(bf16[256,5120]{1,0:T(8,128)(2,1)S(1)} %copy-done, f32[1,5120]{1,0:T(1,128)S(1)} %bitcast.4), custom_call_target="tpu_custom_call" | custom-call | flops 8000000 | bytes 5300000 | tf_op jit(solution)/shard_map/norm_text/pallas_call | solution.py:271
  26.7 9.1 %all-to-all-done.parts = bf16[16,32,896]{2,1,0:T(8,128)(2,1)S(1)} async-done(((bf16[16,32,896]{2,1,0:T(8,128)(2,1)}), bf16[16,32,896]{2,1,0:T(8,128)(2,1)S(1)}, u32[]{:S(2)}, u32[]{:S(2)}) %all-to-all-start) | async-done | bytes 917536 | tf_op jit(solution)/shard_map/all_to_all | solution.py:350
  35.9 0.0 copy-start.1
  35.9 0.0 collective-permute-done.w2
  35.9 2.9 %collective-permute-start.3 = (bf16[768,640]{1,0:T(8,128)(2,1)}, bf16[768,640]{1,0:T(8,128)(2,1)S(1)}, u32[]{:S(2)}, u32[]{:S(2)}) collective-permute-start(bf16[768,640]{1,0:T(8,128)(2,1)} %collective-permute-done.w2), channel_id=1, source_target_pairs={{0,16},{16,0},{32,48},{48,32},{64,80},{80,64},{96,112},{112,96},{1... | collective-permute-start | bytes 2949128 | tf_op jit(solution)/shard_map/ppermute | solution.py:341
  38.7 0.0 copy-done.9
  38.7 0.0 copy-done.10
  38.8 0.0 copy-start.2
  38.8 1.3 %copy-done.2 = bf16[768,768]{1,0:T(8,128)(2,1)S(1)} copy-done((bf16[768,768]{1,0:T(8,128)(2,1)S(1)}, bf16[768,768]{1,0:T(8,128)(2,1)}, u32[]{:S(2)}) %copy-start.2) | copy-done | bytes 1179672
  40.0 0.0 copy-start.7
  40.0 0.8 %copy-done.7 = bf16[32,768]{1,0:T(8,128)(2,1)S(1)} copy-done((bf16[32,768]{1,0:T(8,128)(2,1)S(1)}, bf16[32,768]{1,0:T(8,128)(2,1)}, u32[]{:S(2)}) %copy-start.7) | copy-done | bytes 49176
  40.8 0.0 copy-start.4
  40.8 1.1 %combine.1.rows = bf16[32,768]{1,0:T(8,128)(2,1)S(1)} custom-call(bf16[16,32,896]{2,1,0:T(8,128)(2,1)S(1)} %all-to-all-done.parts, bf16[32,768]{1,0:T(8,128)(2,1)S(1)} %copy-done.7, bf16[768,768]{1,0:T(8,128)(2,1)S(1)} %copy-done.2, f32[1,768]{1,0:T(1,128)S(1)} %reshape.13.gain, f32[1,768]{1,0:T(1,128)S(1)} %reshape.14.bias), custom_call_target="tpu_custom_call" | custom-call | tf_op jit(solution)/shard_map/combine/pallas_call | solution.py:226
  41.9 2.1 %collective-permute-start.1 = (bf16[32,768]{1,0:T(8,128)(2,1)S(1)}, bf16[32,768]{1,0:T(8,128)(2,1)S(1)}, u32[]{:S(2)}, u32[]{:S(2)}) collective-permute-start(bf16[32,768]{1,0:T(8,128)(2,1)S(1)} %combine.1.rows), channel_id=1, source_target_pairs={{0,96},{16,112},{32,64},{48,80},{64,32},{80,48},{96,0},{112,16},{1... | collective-permute-start | bytes 147464 | tf_op jit(solution)/shard_map/ppermute | solution.py:341
  44.0 0.0 collective-permute-done.2.w1
  44.0 0.0 collective-permute-done.3.w3
  44.0 0.0 copy-done.1
  44.1 0.0 copy-start.3
  44.1 0.7 %copy-done.3 = f32[5120]{0:T(1024)S(1)} copy-done((f32[5120]{0:T(1024)S(1)}, f32[5120]{0:T(1024)}, u32[]{:S(2)}) %copy-start.3) | copy-done | bytes 20504
  44.8 2.2 %project.2.mine = bf16[32,2560]{1,0:T(8,128)(2,1)S(1)} custom-call(bf16[32,768]{1,0:T(8,128)(2,1)S(1)} %combine.1.rows, bf16[768,640]{1,0:T(8,128)(2,1)S(1)} %copy-done.1, bf16[768,640]{1,0:T(8,128)(2,1)} %collective-permute-done.2.w1, bf16[768,640]{1,0:T(8,128)(2,1)} %collective-permute-done.w2, bf16[768,640]{1,0:T(8,128)(2,1)S(1)} %collective-permute-done.3.w3, ...), custom_call_target="tpu_custom_call" | custom-call | flops 126000000 | bytes 4200000 | tf_op jit(solution)/shard_map/project/pallas_call | solution.py:249
  47.0 0.0 copy-start.6
  47.0 0.0 copy-start.8
  47.0 0.0 collective-permute-done.1.rows
  47.0 0.0 copy-done.4
  47.0 2.2 %project.3 = bf16[32,2560]{1,0:T(8,128)(2,1)S(1)} custom-call(bf16[32,768]{1,0:T(8,128)(2,1)S(1)} %collective-permute-done.1.rows, bf16[768,640]{1,0:T(8,128)(2,1)S(1)} %copy-done.1, bf16[768,640]{1,0:T(8,128)(2,1)} %collective-permute-done.2.w1, bf16[768,640]{1,0:T(8,128)(2,1)} %collective-permute-done.w2, bf16[768,640]{1,0:T(8,128)(2,1)S(1)} %collective-permute-done.3.w3, ...), custom_call_target="tpu_custom_call" | custom-call | flops 126000000 | bytes 4200000 | tf_op jit(solution)/shard_map/project/pallas_call | solution.py:249
  49.2 1.2 %collective-permute-start.4 = (bf16[32,2560]{1,0:T(8,128)(2,1)S(1)}, bf16[32,2560]{1,0:T(8,128)(2,1)S(1)}, u32[]{:S(2)}, u32[]{:S(2)}) collective-permute-start(bf16[32,2560]{1,0:T(8,128)(2,1)S(1)} %project.3), channel_id=1, source_target_pairs={{0,96},{16,112},{32,64},{48,80},{64,32},{80,48},{96,0},{112,16},{1... | collective-permute-start | bytes 491528 | tf_op jit(solution)/shard_map/ppermute | solution.py:341
  50.5 5.5 %collective-permute-done.4.other = bf16[32,2560]{1,0:T(8,128)(2,1)S(1)} collective-permute-done((bf16[32,2560]{1,0:T(8,128)(2,1)S(1)}, bf16[32,2560]{1,0:T(8,128)(2,1)S(1)}, u32[]{:S(2)}, u32[]{:S(2)}) %collective-permute-start.4) | collective-permute-done | bytes 163872 | tf_op jit(solution)/shard_map/ppermute | solution.py:341
  56.0 0.0 copy-done.6
  56.0 0.0 copy-done.8
  56.0 2.3 %place.1 = bf16[256,5120]{1,0:T(8,128)(2,1)} custom-call(s32[128]{0:T(128)S(1)} %copy-done.8, bf16[32,2560]{1,0:T(8,128)(2,1)S(1)} %project.2.mine, bf16[32,2560]{1,0:T(8,128)(2,1)S(1)} %collective-permute-done.4.other, f32[1,5120]{1,0:T(1,128)S(1)} %bitcast.5, bf16[256,5120]{1,0:T(8,128)(2,1)S(1)} %copy-done, ...), custom_call_target="tpu_custom_call", output_to_operand_aliasing={{}: (5, {})} | custom-call | tf_op jit(solution)/shard_map/place/pallas_call | solution.py:319
  (2 shorter events, 0.0 us)
Async XLA Ops:
  0.0 35.9 %collective-permute-start = (bf16[768,640]{1,0:T(8,128)(2,1)}, bf16[768,640]{1,0:T(8,128)(2,1)}, u32[]{:S(2)}, u32[]{:S(2)}) collective-permute-start(bf16[768,640]{1,0:T(8,128)(2,1)} %w0.3), channel_id=1, source_target_pairs={{0,32},{16,48},{32,0},{48,16},{64,96},{80,112},{96,64},{112,80},{1... | collective-permute-start | bytes 2949128 | tf_op jit(solution)/shard_map/ppermute | solution.py:341
  2.1 21.1 %copy-start = (bf16[256,5120]{1,0:T(8,128)(2,1)S(1)}, bf16[256,5120]{1,0:T(8,128)(2,1)}, u32[]{:S(2)}) copy-start(bf16[256,5120]{1,0:T(8,128)(2,1)} %text.2) | copy-start | bytes 7864324
  14.4 21.4 %all-to-all-start = ((bf16[16,32,896]{2,1,0:T(8,128)(2,1)}), bf16[16,32,896]{2,1,0:T(8,128)(2,1)S(1)}, u32[]{:S(2)}, u32[]{:S(2)}) async-start(bf16[16,32,896]{2,1,0:T(8,128)(2,1)} %attend.1), calls=%async_computation | async-start | bytes 1835008 | tf_op jit(solution)/shard_map/all_to_all | solution.py:350
  21.9 22.2 %collective-permute-start.2 = (bf16[768,640]{1,0:T(8,128)(2,1)}, bf16[768,640]{1,0:T(8,128)(2,1)}, u32[]{:S(2)}, u32[]{:S(2)}) collective-permute-start(bf16[768,640]{1,0:T(8,128)(2,1)} %w0.3), channel_id=1, source_target_pairs={{0,16},{16,0},{32,48},{48,32},{64,80},{80,64},{96,112},{112,96},{1... | collective-permute-start | bytes 2949128 | tf_op jit(solution)/shard_map/ppermute | solution.py:341
  23.2 0.7 %copy-start.5 = (f32[5120]{0:T(1024)S(1)}, f32[5120]{0:T(1024)}, u32[]{:S(2)}) copy-start(f32[5120]{0:T(1024)} %param.31) | copy-start | bytes 61444
  23.9 14.8 %copy-start.9 = (f32[768]{0:T(1024)S(1)}, f32[768]{0:T(1024)}, u32[]{:S(2)}) copy-start(f32[768]{0:T(1024)} %param.26) | copy-start | bytes 9220
  23.9 14.8 %copy-start.10 = (f32[768]{0:T(1024)S(1)}, f32[768]{0:T(1024)}, u32[]{:S(2)}) copy-start(f32[768]{0:T(1024)} %param.27) | copy-start | bytes 9220
  35.9 8.2 %copy-start.1 = (bf16[768,640]{1,0:T(8,128)(2,1)S(1)}, bf16[768,640]{1,0:T(8,128)(2,1)}, u32[]{:S(2)}) copy-start(bf16[768,640]{1,0:T(8,128)(2,1)} %w0.3) | copy-start | bytes 2949124
  35.9 8.2 %collective-permute-start.3 = (bf16[768,640]{1,0:T(8,128)(2,1)}, bf16[768,640]{1,0:T(8,128)(2,1)S(1)}, u32[]{:S(2)}, u32[]{:S(2)}) collective-permute-start(bf16[768,640]{1,0:T(8,128)(2,1)} %collective-permute-done.w2), channel_id=1, source_target_pairs={{0,16},{16,0},{32,48},{48,32},{64,80},{80,64},{96,112},{112,96},{1... | collective-permute-start | bytes 2949128 | tf_op jit(solution)/shard_map/ppermute | solution.py:341
  38.8 1.3 %copy-start.2 = (bf16[768,768]{1,0:T(8,128)(2,1)S(1)}, bf16[768,768]{1,0:T(8,128)(2,1)}, u32[]{:S(2)}) copy-start(bf16[768,768]{1,0:T(8,128)(2,1)} %w_out.1) | copy-start | bytes 3538948
  40.0 0.8 %copy-start.7 = (bf16[32,768]{1,0:T(8,128)(2,1)S(1)}, bf16[32,768]{1,0:T(8,128)(2,1)}, u32[]{:S(2)}) copy-start(bf16[32,768]{1,0:T(8,128)(2,1)} %queries.1) | copy-start | bytes 147460
  40.8 6.2 %copy-start.4 = (f32[5120]{0:T(1024)S(1)}, f32[5120]{0:T(1024)}, u32[]{:S(2)}) copy-start(f32[5120]{0:T(1024)} %param.29) | copy-start | bytes 61444
  41.9 5.1 %collective-permute-start.1 = (bf16[32,768]{1,0:T(8,128)(2,1)S(1)}, bf16[32,768]{1,0:T(8,128)(2,1)S(1)}, u32[]{:S(2)}, u32[]{:S(2)}) collective-permute-start(bf16[32,768]{1,0:T(8,128)(2,1)S(1)} %combine.1.rows), channel_id=1, source_target_pairs={{0,96},{16,112},{32,64},{48,80},{64,32},{80,48},{96,0},{112,16},{1... | collective-permute-start | bytes 147464 | tf_op jit(solution)/shard_map/ppermute | solution.py:341
  44.1 0.7 %copy-start.3 = (f32[5120]{0:T(1024)S(1)}, f32[5120]{0:T(1024)}, u32[]{:S(2)}) copy-start(f32[5120]{0:T(1024)} %param.29) | copy-start | bytes 61444
  47.0 9.0 %copy-start.6 = (f32[5120]{0:T(1024)S(1)}, f32[5120]{0:T(1024)}, u32[]{:S(2)}) copy-start(f32[5120]{0:T(1024)} %param.31) | copy-start | bytes 61444
  47.0 9.0 %copy-start.8 = (s32[128]{0:T(128)S(1)}, s32[128]{0:T(128)}, u32[]{:S(2)}) copy-start(s32[128]{0:T(128)} %starts.1) | copy-start | bytes 1540
  49.2 6.7 %collective-permute-start.4 = (bf16[32,2560]{1,0:T(8,128)(2,1)S(1)}, bf16[32,2560]{1,0:T(8,128)(2,1)S(1)}, u32[]{:S(2)}, u32[]{:S(2)}) collective-permute-start(bf16[32,2560]{1,0:T(8,128)(2,1)S(1)} %project.3), channel_id=1, source_target_pairs={{0,96},{16,112},{32,64},{48,80},{64,32},{80,48},{96,0},{112,16},{1... | collective-permute-start | bytes 491528 | tf_op jit(solution)/shard_map/ppermute | solution.py:341

commit v2 on v1

v2 whole, which is shorter than its diff:
```python
import math

import jax
import jax.numpy as jnp
from jax import lax
from jax.experimental import pallas as pl
from jax.experimental.pallas import tpu as pltpu
from jax.sharding import PartitionSpec as P

HEADS = 12
HD = 64
WIDTH = HEADS * HD
VQ = 32
QF = 32
DL = 5120
SLOTS = 4
COLUMNS = 16
BLOCK = 256
SHARE = DL // 8
WINDOW = 48
STATS = 128
CHUNK = 8
NEAR = 6
MERGE_VMEM = 66_100_000
GROUP = 4
NEG = -1e30
MIB = 1 << 20

f32 = jnp.float32
bf16 = jnp.bfloat16


def iota(shape, axis):
    return lax.broadcasted_iota(jnp.int32, shape, axis)


def attend_kernel(
    selected_in, counts_in, starts_in, frames, pos_in, queries_in, w_query_in, w_key_in, w_value_in, out,
    selected, counts, starts, pos, queries, w_query, w_key, w_value, x_raw, x_keys, scores, values,
    folded, pos_wide, staged, scalar_sems, sems, weight_sems, out_sems,
):
    row = lax.axis_index("tm")
    column = lax.axis_index("video")
    scalars = [
        pltpu.make_async_copy(source, target, scalar_sems.at[i])
        for i, (source, target) in enumerate(
            ((selected_in, selected), (counts_in, counts), (starts_in, starts))
        )
    ]
    loads = [
        pltpu.make_async_copy(source, target, weight_sems.at[i])
        for i, (source, target) in enumerate((
            (queries_in, queries), (w_query_in, w_query), (w_key_in, w_key), (pos_in, pos),
            (w_value_in, w_value),
        ))
    ]
    for copy in scalars + loads:
        copy.start()
    for copy in scalars:
        copy.wait()

    def slot(video, j):
        count = counts[video]
        last = jnp.maximum(count >> 4, 1) - 1
        k = ((column * count) >> 4) + jnp.minimum(j, last)
        frame = selected[video, k] - column * 8
        live = (j <= last) & (frame >= 0) & (frame < 8)
        return k, jnp.clip(frame, 0, 7), live

    def fetch(video):
        for j in range(SLOTS):
            _, frame, _ = slot(video, j)
            pltpu.make_async_copy(
                frames.at[video, frame], x_raw.at[video * SLOTS + j], sems.at[video]
            ).start()

    pl.loop(0, COLUMNS)(fetch)
    for copy in loads[:2]:
        copy.wait()
    query = jnp.dot(queries[...], w_query[...], preferred_element_type=f32).astype(bf16)
    query = query * jnp.asarray(1.0 / math.sqrt(HD), bf16)
    loads[2].wait()
    for g in range(HEADS // GROUP):
        wide = GROUP * HD
        part = query[:, g * wide:(g + 1) * wide]
        part = jnp.concatenate([part] * GROUP, axis=0)
        same = iota(part.shape, 0) // VQ == iota(part.shape, 1) // HD
        part = jnp.where(same, part, jnp.zeros_like(part))
        fold = lax.dot_general(
            part, w_key[:, g * wide:(g + 1) * wide], (((1,), (1,)), ((), ())),
            preferred_element_type=f32,
        )
        rows = GROUP * VQ
        folded[g * rows:(g + 1) * rows, :] = fold.astype(bf16)
    loads[3].wait()
    pos_wide[...] = pos[...].astype(f32)

    lane = iota((VQ, STATS), 1)
    stat_head = lane % HEADS
    stat_part = lane // HEADS
    piece = stat_part % 3

    keys = SLOTS * QF

    def wait(chunk):
        for t in range(CHUNK):
            video = chunk * CHUNK + t
            pltpu.make_async_copy(
                frames.at[video, pl.ds(0, SLOTS)], x_raw.at[pl.ds(video * SLOTS, SLOTS)], sems.at[video]
            ).wait()

    def add(chunk, x_keys):
        for t in range(CHUNK):
            video = chunk * CHUNK + t
            for j in range(SLOTS):
                k, _, _ = slot(video, j)
                x = x_raw[video * SLOTS + j].astype(f32) + pos_wide[pl.ds(k, 1), :]
                at = (t * SLOTS + j) * QF
                x_keys[at:at + QF, :] = x.astype(bf16)

    def score(x_keys, scores, values):
        x = x_keys[...]
        scores[...] = lax.dot_general(folded[...], x, (((1,), (1,)), ((), ())), preferred_element_type=f32)
        values[...] = jnp.dot(x, w_value[...], preferred_element_type=f32).astype(bf16)

    def send(video):
        block = ((starts[row * COLUMNS + video] - row * (COLUMNS * BLOCK)) >> 8) & (COLUMNS - 1)
        return pltpu.make_async_copy(staged.at[video], out.at[block], out_sems.at[video])

    def finish(chunk, scores, values):
        for t in range(CHUNK):
            video = chunk * CHUNK + t
            alive = jnp.int32(0)
            for j in range(SLOTS):
                alive = alive + slot(video, j)[2].astype(jnp.int32)
            hidden = jnp.where(iota((1, keys), 1) < alive * QF, 0.0, NEG)
            s = scores[:, t * keys:(t + 1) * keys] + hidden
            top = jnp.max(s, axis=1, keepdims=True)
            p = jnp.exp(s - top)
            total = jnp.sum(p, axis=1, keepdims=True)
            p = p.astype(bf16)
            for g in range(HEADS // GROUP):
                wide = GROUP * HD
                rows = GROUP * VQ
                full = jnp.dot(
                    p[g * rows:(g + 1) * rows], values[t * keys:(t + 1) * keys, g * wide:(g + 1) * wide],
                    preferred_element_type=f32,
                )
                head = iota((VQ, wide), 1) // HD
                context = full[:VQ]
                for h in range(1, GROUP):
                    context = jnp.where(head == h, full[h * VQ:(h + 1) * VQ], context)
                staged[video, :, g * wide:(g + 1) * wide] = context.astype(bf16)
            stat = jnp.zeros((VQ, STATS), f32)
            for h in range(HEADS):
                one = jnp.where(stat_part < 3, top[h * VQ:(h + 1) * VQ], total[h * VQ:(h + 1) * VQ])
                stat = jnp.where(stat_head == h, one, stat)
            high = stat.astype(bf16).astype(f32)
            mid = (stat - high).astype(bf16).astype(f32)
            low = stat - high - mid
            stat = jnp.where(piece == 0, high, jnp.where(piece == 1, mid, low))
            stat = jnp.where(stat_part < 6, stat, 0.0)
            staged[video, :, WIDTH:] = stat.astype(bf16)

    chunks = COLUMNS // CHUNK
    wait(0)
    add(0, x_keys.at[0])
    loads[4].wait()
    for chunk in range(chunks + 1):
        if chunk + 1 < chunks:
            wait(chunk + 1)
        if chunk < chunks:
            score(x_keys.at[chunk % 2], scores.at[chunk % 2], values.at[chunk % 2])
        if chunk + 1 < chunks:
            add(chunk + 1, x_keys.at[(chunk + 1) % 2])
        if chunk > 0:
            finish(chunk - 1, scores.at[(chunk - 1) % 2], values.at[(chunk - 1) % 2])
        if chunk > 0:
            for t in range(CHUNK):
                send((chunk - 1) * CHUNK + t).start()
    for video in range(COLUMNS):
        send(video).wait()


def attend(selected, counts, starts, frames, pos, queries, w_query, w_key, w_value):
    return pl.pallas_call(
        attend_kernel,
        out_shape=jax.ShapeDtypeStruct((COLUMNS, VQ, WIDTH + STATS), bf16),
        in_specs=[pl.BlockSpec(memory_space=pl.ANY)] * 9,
        out_specs=pl.BlockSpec(memory_space=pl.ANY),
        scratch_shapes=[
            pltpu.SMEM(selected.shape, jnp.int32),
            pltpu.SMEM(counts.shape, jnp.int32),
            pltpu.SMEM(starts.shape, jnp.int32),
            pltpu.VMEM(pos.shape, bf16),
            pltpu.VMEM(queries.shape, bf16),
            pltpu.VMEM((WIDTH, WIDTH), bf16),
            pltpu.VMEM((WIDTH, WIDTH), bf16),
            pltpu.VMEM((WIDTH, WIDTH), bf16),
            pltpu.VMEM((COLUMNS * SLOTS, QF, WIDTH), bf16),
            pltpu.VMEM((2, CHUNK * SLOTS * QF, WIDTH), bf16),
            pltpu.VMEM((2, HEADS * VQ, CHUNK * SLOTS * QF), f32),
            pltpu.VMEM((2, CHUNK * SLOTS * QF, WIDTH), bf16),
            pltpu.VMEM((HEADS * VQ, WIDTH), bf16),
            pltpu.VMEM(pos.shape, f32),
            pltpu.VMEM((COLUMNS, VQ, WIDTH + STATS), bf16),
            pltpu.SemaphoreType.DMA((3,)),
            pltpu.SemaphoreType.DMA((COLUMNS,)),
            pltpu.SemaphoreType.DMA((5,)),
            pltpu.SemaphoreType.DMA((COLUMNS,)),
        ],
        compiler_params=pltpu.CompilerParams(vmem_limit_bytes=60 * MIB),
        cost_estimate=pl.CostEstimate(
            flops=9_000_000_000, bytes_accessed=8_000_000, transcendentals=800_000
        ),
        name="attend",
    )(selected, counts, starts, frames, pos, queries, w_query, w_key, w_value)


def nearer(device):
    return device ^ (2 + 4 * (device & 1))


def crossing(device):
    return device ^ (7 - 4 * (device & 1))


def blocks_of(device):
    twin = device ^ 1
    return (
        device, twin, nearer(device) ^ 1, nearer(twin) ^ 1, nearer(device), device ^ 4, nearer(twin), device ^ 5
    )


def window_of(starts):
    row = lax.axis_index("tm")
    column = lax.axis_index("video")
    first = (row * COLUMNS + column) * BLOCK
    offset = jnp.int32(0)
    for w in range(COLUMNS):
        at = starts[row * COLUMNS + w] - first
        offset = offset + jnp.where((at >= 0) & (at < BLOCK), at, 0)
    begin = pl.multiple_of(jnp.minimum(offset >> 4, (BLOCK - WINDOW) // 16) * 16, 16)
    return begin, offset - begin


def merge_kernel(
    parts_in, queries_in, w_out_in, gain_in, bias_in, starts_in, proj_bias_in, text, w0, w1, w2, w3, w4, w5,
    rows_out, wide_out, rest_out,
    parts, queries, w_out, gain, bias, starts, proj_bias, weights, window, sems, weight_sems,
):
    loads = [
        pltpu.make_async_copy(source, target, sems.at[i])
        for i, (source, target) in enumerate((
            (starts_in, starts), (parts_in, parts), (w_out_in, w_out), (queries_in, queries), (gain_in, gain),
            (bias_in, bias), (proj_bias_in, proj_bias),
        ))
    ]
    blocks = [
        pltpu.make_async_copy(source, weights.at[i], weight_sems.at[i])
        for i, source in enumerate((w0, w1, w2, w3, w4, w5))
    ]
    for copy in loads + blocks:
        copy.start()
    loads[0].wait()
    begin, shift = window_of(starts)
    fetch = pltpu.make_async_copy(text.at[pl.ds(begin, WINDOW)], window, sems.at[7])
    fetch.start()
    loads[1].wait()
    stat = parts[:, :, WIDTH:].astype(f32).reshape(COLUMNS * VQ, STATS)

    def shifted(n):
        return pltpu.roll(stat, STATS - n * HEADS, 1)

    tops = stat + shifted(1) + shifted(2)
    totals = shifted(3) + shifted(4) + shifted(5)
    lane = iota((VQ, STATS), 1)
    real = lane < HEADS
    tops = [jnp.where(real, tops[c * VQ:(c + 1) * VQ], 0.0) for c in range(COLUMNS)]
    totals = [jnp.where(real, totals[c * VQ:(c + 1) * VQ], 1.0) for c in range(COLUMNS)]
    top = tops[0]
    for c in range(1, COLUMNS):
        top = jnp.maximum(top, tops[c])
    scales = [jnp.exp(t - top) for t in tops]
    total = scales[0] * totals[0]
    for c in range(1, COLUMNS):
        total = total + scales[c] * totals[c]
    inverse = jnp.where(real, 1.0 / total, 0.0)
    weight = jnp.concatenate([s * inverse for s in scales], axis=0)
    high = weight.astype(bf16)
    low = (weight - high.astype(f32)).astype(bf16)
    spread = (iota((2 * STATS, WIDTH), 0) % STATS == iota((2 * STATS, WIDTH), 1) // HD).astype(f32).astype(bf16)
    weight = jnp.dot(jnp.concatenate([high, low], axis=1), spread, preferred_element_type=f32)
    context = jnp.zeros((VQ, WIDTH), f32)
    for c in range(COLUMNS):
        context = context + weight[c * VQ:(c + 1) * VQ] * parts[c, :, :WIDTH].astype(f32)
    for copy in loads[2:]:
        copy.wait()
    residual = jnp.dot(context.astype(bf16), w_out[...], preferred_element_type=f32) + queries[...].astype(f32)
    mean = jnp.mean(residual, axis=-1, keepdims=True)
    centred = residual - mean
    variance = jnp.mean(centred * centred, axis=-1, keepdims=True)
    rows = (centred * lax.rsqrt(variance + 1e-12) * gain[...] + bias[...]).astype(bf16)
    pick = (iota((WINDOW, VQ), 0) - shift == iota((WINDOW, VQ), 1)).astype(f32).astype(bf16)
    rows = jnp.dot(pick, rows, preferred_element_type=f32).astype(bf16)
    rows_out[...] = rows
    place = iota((WINDOW, SHARE), 0) - shift
    inside = (place >= 0) & (place < VQ)
    fetch.wait()
    for i, block in enumerate(blocks_of(lax.axis_index("tm"))):
        here = pl.ds(pl.multiple_of(block * SHARE, 128), SHARE)
        text_rows = window[:, here]
        if i < NEAR:
            blocks[i].wait()
            result = jnp.dot(rows, weights[i], preferred_element_type=f32) + proj_bias[:, here]
            wide_out[:, i * SHARE:(i + 1) * SHARE] = jnp.where(
                inside, result, text_rows.astype(f32)
            ).astype(bf16)
        else:
            rest_out[:, (i - NEAR) * SHARE:(i - NEAR + 1) * SHARE] = text_rows


def merge(parts, queries, w_out, gain, bias, starts, proj_bias, text, weights):
    vmem = pl.BlockSpec(memory_space=pltpu.VMEM)
    anywhere = pl.BlockSpec(memory_space=pl.ANY)
    return pl.pallas_call(
        merge_kernel,
        out_shape=[
            jax.ShapeDtypeStruct((WINDOW, WIDTH), bf16),
            jax.ShapeDtypeStruct((WINDOW, NEAR * SHARE), bf16),
            jax.ShapeDtypeStruct((WINDOW, DL - NEAR * SHARE), bf16),
        ],
        in_specs=[anywhere] * 14,
        out_specs=[vmem, vmem, vmem],
        scratch_shapes=[
            pltpu.VMEM(parts.shape, bf16),
            pltpu.VMEM(queries.shape, bf16),
            pltpu.VMEM((WIDTH, WIDTH), bf16),
            pltpu.VMEM((1, WIDTH), f32),
            pltpu.VMEM((1, WIDTH), f32),
            pltpu.SMEM(starts.shape, jnp.int32),
            pltpu.VMEM((1, DL), f32),
            pltpu.VMEM((NEAR, WIDTH, SHARE), bf16),
            pltpu.VMEM((WINDOW, DL), bf16),
            pltpu.SemaphoreType.DMA((8,)),
            pltpu.SemaphoreType.DMA((NEAR,)),
        ],
        compiler_params=pltpu.CompilerParams(vmem_limit_bytes=MERGE_VMEM),
        cost_estimate=pl.CostEstimate(flops=500_000_000, bytes_accessed=9_000_000, transcendentals=70_000),
        name="merge",
    )(parts, queries, w_out, gain, bias, starts, proj_bias, text, *weights)


def place_kernel(
    rows_in, wide_in, rest_in, starts_in, proj_bias_in, norm_gain_in, normed, w6, w7, done,
    starts, proj_bias, norm_gain, weights, wide, done_rows, sems, weight_sems,
):
    loads = [
        pltpu.make_async_copy(source, target, sems.at[i])
        for i, (source, target) in enumerate((
            (starts_in, starts), (proj_bias_in, proj_bias), (norm_gain_in, norm_gain),
        ))
    ]
    blocks = [
        pltpu.make_async_copy(source, weights.at[i], weight_sems.at[i]) for i, source in enumerate((w6, w7))
    ]
    for copy in loads + blocks:
        copy.start()
    rows = rows_in[...]
    squares = jnp.zeros((WINDOW, 1), f32)
    all_blocks = blocks_of(lax.axis_index("tm"))
    for i, block in enumerate(all_blocks):
        here = pl.ds(pl.multiple_of(block * SHARE, 128), SHARE)
        if i < NEAR:
            embeds = wide_in[:, i * SHARE:(i + 1) * SHARE].astype(f32)
        else:
            if i == NEAR:
                loads[0].wait()
                begin, shift = window_of(starts)
                place = iota((WINDOW, SHARE), 0) - shift
                inside = (place >= 0) & (place < VQ)
                loads[1].wait()
            blocks[i - NEAR].wait()
            result = jnp.dot(rows, weights[i - NEAR], preferred_element_type=f32) + proj_bias[:, here]
            text_rows = rest_in[:, (i - NEAR) * SHARE:(i - NEAR + 1) * SHARE]
            embeds = jnp.where(inside, result, text_rows.astype(f32)).astype(bf16).astype(f32)
        wide[:, i * SHARE:(i + 1) * SHARE] = embeds
        squares = squares + jnp.sum(embeds * embeds, axis=-1, keepdims=True)
    scale = lax.rsqrt(squares * (1.0 / DL) + 1e-05)
    loads[2].wait()
    for i, block in enumerate(all_blocks):
        here = pl.ds(pl.multiple_of(block * SHARE, 128), SHARE)
        done_rows[:, here] = (wide[:, i * SHARE:(i + 1) * SHARE] * scale * norm_gain[:, here]).astype(bf16)
    store = pltpu.make_async_copy(done_rows, done.at[pl.ds(begin, WINDOW)], sems.at[3])
    store.start()
    store.wait()


def place(rows, wide, rest, starts, proj_bias, norm_gain, normed, weights):
    vmem = pl.BlockSpec(memory_space=pltpu.VMEM)
    anywhere = pl.BlockSpec(memory_space=pl.ANY)
    return pl.pallas_call(
        place_kernel,
        out_shape=jax.ShapeDtypeStruct(normed.shape, bf16),
        in_specs=[vmem] * 3 + [anywhere] * 6,
        out_specs=anywhere,
        input_output_aliases={6: 0},
        scratch_shapes=[
            pltpu.SMEM(starts.shape, jnp.int32),
            pltpu.VMEM((1, DL), f32),
            pltpu.VMEM((1, DL), f32),
            pltpu.VMEM((8 - NEAR, WIDTH, SHARE), bf16),
            pltpu.VMEM((WINDOW, DL), f32),
            pltpu.VMEM((WINDOW, DL), bf16),
            pltpu.SemaphoreType.DMA((4,)),
            pltpu.SemaphoreType.DMA((8 - NEAR,)),
        ],
        compiler_params=pltpu.CompilerParams(vmem_limit_bytes=MERGE_VMEM),
        name="place",
    )(rows, wide, rest, starts, proj_bias, norm_gain, normed, *weights)


def norm_rows(wide, gain):
    squares = jnp.mean(wide * wide, axis=-1, keepdims=True)
    return (wide * lax.rsqrt(squares + 1e-05) * gain).astype(bf16)


def text_kernel(text, gain, out):
    out[...] = norm_rows(text[...].astype(f32), gain[...])


def norm_text(text, gain):
    rows = 64
    return pl.pallas_call(
        text_kernel,
        out_shape=jax.ShapeDtypeStruct(text.shape, bf16),
        grid=(text.shape[0] // rows,),
        in_specs=[
            pl.BlockSpec((rows, DL), lambda i: (i, 0)),
            pl.BlockSpec((1, DL), lambda i: (0, 0)),
        ],
        out_specs=pl.BlockSpec((rows, DL), lambda i: (i, 0)),
        compiler_params=pltpu.CompilerParams(vmem_limit_bytes=24 * MIB),
        cost_estimate=pl.CostEstimate(flops=8_000_000, bytes_accessed=5_300_000, transcendentals=256),
        name="norm_text",
    )(text, gain)


def per_device(
    frame_feats, selected, counts, video_start, queries, frame_pos, w_query, w_key, w_value, w_out,
    ln_gain, ln_bias, proj_weight, proj_bias, text_embeds, norm_gain,
):
    def move(x, target):
        return lax.ppermute(x, "tm", [(k, target(k)) for k in range(8)])

    def twin_of(device):
        return device ^ 1

    near_twin = move(proj_weight, crossing)
    twin = move(proj_weight, twin_of)
    parts = attend(
        selected, counts, video_start, frame_feats, frame_pos, queries, w_query, w_key, w_value
    )
    gain = norm_gain.reshape(1, DL)
    bias = proj_bias.reshape(1, DL)
    parts, text, share = lax.optimization_barrier((parts, text_embeds, proj_weight))
    far = move(near_twin, crossing)
    near = move(share, nearer)
    received = lax.all_to_all(parts, "video", split_axis=0, concat_axis=0, tiled=True)
    normed = norm_text(text, gain)
    ln_gain, ln_bias = ln_gain.reshape(1, WIDTH), ln_bias.reshape(1, WIDTH)
    received, normed, near, far, ln_gain, ln_bias, bias = lax.optimization_barrier(
        (received, normed, near, far, ln_gain, ln_bias, bias)
    )
    other_near_twin = move(near_twin, twin_of)
    other_near, far_twin = move(near, twin_of), move(far, twin_of)
    rows, wide, rest = merge(
        received, queries, w_out, ln_gain, ln_bias, video_start, bias, text_embeds,
        (proj_weight, twin, near_twin, other_near_twin, near, far),
    )
    rows, wide, rest, other_near, far_twin = lax.optimization_barrier((rows, wide, rest, other_near, far_twin))
    return place(rows, wide, rest, video_start, bias, gain, normed, (other_near, far_twin))


def solution(mesh):
    in_specs = (
        P("tm", "video", None, None), P("tm", None), P("tm"), P(), P(), P(), P(), P(), P(), P(),
        P(), P(), P(None, "tm"), P(), P(("tm", "video"), None), P(),
    )
    return jax.shard_map(
        per_device, mesh=mesh, in_specs=in_specs, out_specs=P(("tm", "video"), None), check_vma=False
    )
```

time: 58.6 us -> 52.2 us (0.89)
  waiting for transfers between devices: 14.6 us -> 8.51 us
  starting transfers between devices: 17.1 us -> 19.6 us
  local copies, waits for them, and re-layouts: 3.55 us -> 1.2 us
  Pallas kernels: 22.8 us -> 22.2 us
    all_to_all x1, waiting for transfers between devices: 9.12 us -> 3.74 us  [per_device(): lax.all_to_all(parts, 'video', split_axis=0, concat_axis=0, tiled=True)]
    unnamed x22 -> x8, local copies, waits for them, and re-layouts: 3.54 us -> 0.01 us
    pallas_call x1, Pallas kernels: 12.3 us -> 9.04 us  [attend(): pl.pallas_call(attend_kernel, out_shape=jax.ShapeDtypeStruct((COLUMNS, VQ...]
    ppermute x5 -> x7, starting transfers between devices: 9.69 us -> 12 us  [move(): return lax.ppermute(x, 'tm', [(k, target(k)) for k in range(8)])]
    pallas_call x1, Pallas kernels: 2.27 us -> 3.99 us  [place(): pl.pallas_call(place_kernel, out_shape=jax.ShapeDtypeStruct(normed.shape,...]
    reshape x2, local copies, waits for them, and re-layouts: 0.01 us -> 1.18 us  [per_device(): ln_gain, ln_bias = (ln_gain.reshape(1, WIDTH), ln_bias.reshape(1, WIDTH))]
    pallas_call x3 -> x1, Pallas kernels: 5.47 us -> 6.35 us  [merge(): pl.pallas_call(merge_kernel, out_shape=[jax.ShapeDtypeStruct((WINDOW, WID...]
    ppermute x5 -> x7, waiting for transfers between devices: 5.49 us -> 4.77 us  [move(): return lax.ppermute(x, 'tm', [(k, target(k)) for k in range(8)])]
  transfers between devices with their start and end apart: 6 -> 8, of which waited for: 2 -> 3; matrix products, arithmetic and copies ran while one was open for 0% -> 2% of each run, Pallas kernels for 32% -> 35%
where the time goes in v2:
time: 52.2 us; the launch traced here: 51.5 us
  Pallas kernels  22.2 us (43%)
  starting transfers between devices  19.6 us (38%)
  waiting for transfers between devices  8.51 us (16%)
  local copies, waits for them, and re-layouts  1.2 us (2%)
    ppermute x7, starting transfers between devices, move(): return lax.ppermute(x, 'tm', [(k, target(k)) for k in range(8)])  12 us
    pallas_call x1, Pallas kernels, attend(): pl.pallas_call(attend_kernel, out_shape=jax.ShapeDtypeStruct((COLUMNS, VQ...  9.04 us
    all_to_all x1, starting transfers between devices, per_device(): lax.all_to_all(parts, 'video', split_axis=0, concat_axis=0, tiled=True)  7.64 us
    pallas_call x1, Pallas kernels, merge(): pl.pallas_call(merge_kernel, out_shape=[jax.ShapeDtypeStruct((WINDOW, WID...  6.35 us
    ppermute x7, waiting for transfers between devices, move(): return lax.ppermute(x, 'tm', [(k, target(k)) for k in range(8)])  4.77 us
    pallas_call x1, Pallas kernels, place(): pl.pallas_call(place_kernel, out_shape=jax.ShapeDtypeStruct(normed.shape,...  3.99 us
    all_to_all x1, waiting for transfers between devices, per_device(): lax.all_to_all(parts, 'video', split_axis=0, concat_axis=0, tiled=True)  3.74 us
    pallas_call x1, Pallas kernels, norm_text(): pl.pallas_call(text_kernel, out_shape=jax.ShapeDtypeStruct(text.shape, bf...  2.8 us
  transfers between devices with their start and end apart: 8, of which 3 were waited for; matrix products, arithmetic and copies ran while one was open for 2% of the time, Pallas kernels for 35%

profile of v2, /device:TPU:1, one launch (start us, length us, event | category | flops | bytes accessed | tf_op | source)
XLA Modules:
  0.0 51.5 jit_solution(4485523851388841459)
XLA Ops:
  0.0 0.0 copy-start.2
  0.0 0.0 copy-start.3
  0.0 0.0 copy-start.1
  0.0 2.8 %collective-permute-start.1 = (bf16[768,640]{1,0:T(8,128)(2,1)}, bf16[768,640]{1,0:T(8,128)(2,1)}, u32[]{:S(2)}, u32[]{:S(2)}) collective-permute-start(bf16[768,640]{1,0:T(8,128)(2,1)} %w0.1), channel_id=1, source_target_pairs={{0,112},{16,32},{32,80},{48,0},{64,48},{80,96},{96,16},{112,64},{1... | collective-permute-start | bytes 2949128 | tf_op jit(solution)/shard_map/ppermute | solution.py:454
  2.8 0.0 copy-start
  2.8 9.0 %attend.1 = bf16[16,32,896]{2,1,0:T(8,128)(2,1)} custom-call(s32[16,64]{1,0:T(8,128)} %selected_in.1, s32[16]{0:T(128)} %counts_in.1, s32[128]{0:T(128)} %starts_in.5, bf16[16,8,32,768]{3,2,1,0:T(8,128)(2,1)} %frames.1, bf16[64,768]{1,0:T(8,128)(2,1)} %pos_in.1, bf16[32,768]{1,0:T(8,128)(2,1)} %queries_in.3, bf16[768,768]{1,0:T(8,128)(2,1)} %w_query_in.1, ...), custom_call_target="tpu_custom_call" | custom-call | flops 8999999488 | bytes 8000000 | tf_op jit(solution)/shard_map/attend/pallas_call | solution.py:186
  11.8 2.0 %collective-permute-start = (bf16[768,640]{1,0:T(8,128)(2,1)}, bf16[768,640]{1,0:T(8,128)(2,1)}, u32[]{:S(2)}, u32[]{:S(2)}) collective-permute-start(bf16[768,640]{1,0:T(8,128)(2,1)} %w0.1), channel_id=1, source_target_pairs={{0,32},{16,112},{32,0},{48,80},{64,96},{80,48},{96,64},{112,16},{1... | collective-permute-start | bytes 2949128 | tf_op jit(solution)/shard_map/ppermute | solution.py:454
  13.8 2.9 %collective-permute-done.1.w2 = bf16[768,640]{1,0:T(8,128)(2,1)} collective-permute-done((bf16[768,640]{1,0:T(8,128)(2,1)}, bf16[768,640]{1,0:T(8,128)(2,1)}, u32[]{:S(2)}, u32[]{:S(2)}) %collective-permute-start.1) | collective-permute-done | bytes 983072 | tf_op jit(solution)/shard_map/ppermute | solution.py:454
  16.7 0.0 collective-permute-start.2
  16.7 7.6 %all-to-all-start = ((bf16[16,32,896]{2,1,0:T(8,128)(2,1)}), bf16[16,32,896]{2,1,0:T(8,128)(2,1)}, u32[]{:S(2)}, u32[]{:S(2)}) async-start(bf16[16,32,896]{2,1,0:T(8,128)(2,1)} %attend.1), calls=%async_computation | async-start | bytes 1835008 | tf_op jit(solution)/shard_map/all_to_all | solution.py:469
  24.4 3.6 %collective-permute-start.3 = (bf16[768,640]{1,0:T(8,128)(2,1)}, bf16[768,640]{1,0:T(8,128)(2,1)}, u32[]{:S(2)}, u32[]{:S(2)}) collective-permute-start(bf16[768,640]{1,0:T(8,128)(2,1)} %w0.1), channel_id=1, source_target_pairs={{0,16},{16,0},{32,48},{48,32},{64,80},{80,64},{96,112},{112,96},{1... | collective-permute-start | bytes 2949128 | tf_op jit(solution)/shard_map/ppermute | solution.py:454
  28.0 0.1 collective-permute-start.4
  28.1 0.0 copy-done.2
  28.1 0.6 %reshape.13.gain_in = f32[1,768]{1,0:T(1,128)} reshape(f32[768]{0:T(1024)S(1)} %copy-done.2) | data formatting | bytes 6144 | tf_op jit(solution)/shard_map/reshape | solution.py:471
  28.6 0.0 copy-done.3
  28.6 0.6 %reshape.14.bias_in = f32[1,768]{1,0:T(1,128)} reshape(f32[768]{0:T(1024)S(1)} %copy-done.3) | data formatting | bytes 6144 | tf_op jit(solution)/shard_map/reshape | solution.py:471
  29.2 0.0 copy-done.1
  29.2 0.0 copy-done
  29.2 2.8 %norm_text.1.normed = bf16[256,5120]{1,0:T(8,128)(2,1)} custom-call(bf16[256,5120]{1,0:T(8,128)(2,1)S(1)} %copy-done, f32[1,5120]{1,0:T(1,128)S(1)} %bitcast.3), custom_call_target="tpu_custom_call" | custom-call | flops 8000000 | bytes 5300000 | tf_op jit(solution)/shard_map/norm_text/pallas_call | solution.py:434
  32.0 3.7 %all-to-all-done.parts_in = bf16[16,32,896]{2,1,0:T(8,128)(2,1)} async-done(((bf16[16,32,896]{2,1,0:T(8,128)(2,1)}), bf16[16,32,896]{2,1,0:T(8,128)(2,1)}, u32[]{:S(2)}, u32[]{:S(2)}) %all-to-all-start) | async-done | bytes 917536 | tf_op jit(solution)/shard_map/all_to_all | solution.py:469
  35.8 0.0 collective-permute-done.w4
  35.8 1.9 %collective-permute-done.2.w5 = bf16[768,640]{1,0:T(8,128)(2,1)} collective-permute-done((bf16[768,640]{1,0:T(8,128)(2,1)}, bf16[768,640]{1,0:T(8,128)(2,1)}, u32[]{:S(2)}, u32[]{:S(2)}) %collective-permute-start.2) | collective-permute-done | bytes 983072 | tf_op jit(solution)/shard_map/ppermute | solution.py:454
  37.7 3.4 %collective-permute-start.5 = (bf16[768,640]{1,0:T(8,128)(2,1)}, bf16[768,640]{1,0:T(8,128)(2,1)}, u32[]{:S(2)}, u32[]{:S(2)}) collective-permute-start(bf16[768,640]{1,0:T(8,128)(2,1)} %collective-permute-done.w4), channel_id=1, source_target_pairs={{0,16},{16,0},{32,48},{48,32},{64,80},{80,64},{96,112},{112,96},{1... | collective-permute-start | bytes 2949128 | tf_op jit(solution)/shard_map/ppermute | solution.py:454
  41.1 0.1 collective-permute-start.6
  41.2 0.0 collective-permute-done.3.w1
  41.2 0.0 collective-permute-done.4.w3
  41.2 6.4 %merge.1 = (bf16[48,768]{1,0:T(8,128)(2,1)}, bf16[48,3840]{1,0:T(8,128)(2,1)}, bf16[48,1280]{1,0:T(8,128)(2,1)}) custom-call(bf16[16,32,896]{2,1,0:T(8,128)(2,1)} %all-to-all-done.parts_in, bf16[32,768]{1,0:T(8,128)(2,1)} %queries_in.3, bf16[768,768]{1,0:T(8,128)(2,1)} %w_out_in.1, f32[1,768]{1,0:T(1,128)} %reshape.13.gain_in, f32[1,768]{1,0:T(1,128)} %reshape.14.bias_in, ...), custom_call_target="tpu_custom_call" | custom-call | flops 500000000 | bytes 9000000 | tf_op jit(solution)/shard_map/merge/pallas_call | solution.py:326
  47.5 0.0 collective-permute-done.5.w6
  47.5 0.0 collective-permute-done.6.w7
  47.6 4.0 %place.1 = bf16[256,5120]{1,0:T(8,128)(2,1)} custom-call(bf16[48,768]{1,0:T(8,128)(2,1)} %get-tuple-element.35.rows_in, bf16[48,3840]{1,0:T(8,128)(2,1)} %get-tuple-element.36.wide_in, bf16[48,1280]{1,0:T(8,128)(2,1)} %get-tuple-element.37.rest_in, s32[128]{0:T(128)} %starts_in.5, f32[1,5120]{1,0:T(1,128)} %bitcast.5, ...), custom_call_target="tpu_custom_call", output_to_operand_aliasing={{}: (6, {})} | custom-call | tf_op jit(solution)/shard_map/place/pallas_call | solution.py:402
Async XLA Ops:
  0.0 28.1 %copy-start.2 = (f32[768]{0:T(1024)S(1)}, f32[768]{0:T(1024)}, u32[]{:S(2)}) copy-start(f32[768]{0:T(1024)} %param.26) | copy-start | bytes 9220
  0.0 28.6 %copy-start.3 = (f32[768]{0:T(1024)S(1)}, f32[768]{0:T(1024)}, u32[]{:S(2)}) copy-start(f32[768]{0:T(1024)} %param.27) | copy-start | bytes 9220
  0.0 29.2 %copy-start.1 = (f32[5120]{0:T(1024)S(1)}, f32[5120]{0:T(1024)}, u32[]{:S(2)}) copy-start(f32[5120]{0:T(1024)} %param.31) | copy-start | bytes 61444
  0.0 16.7 %collective-permute-start.1 = (bf16[768,640]{1,0:T(8,128)(2,1)}, bf16[768,640]{1,0:T(8,128)(2,1)}, u32[]{:S(2)}, u32[]{:S(2)}) collective-permute-start(bf16[768,640]{1,0:T(8,128)(2,1)} %w0.1), channel_id=1, source_target_pairs={{0,112},{16,32},{32,80},{48,0},{64,48},{80,96},{96,16},{112,64},{1... | collective-permute-start | bytes 2949128 | tf_op jit(solution)/shard_map/ppermute | solution.py:454
  2.8 26.5 %copy-start = (bf16[256,5120]{1,0:T(8,128)(2,1)S(1)}, bf16[256,5120]{1,0:T(8,128)(2,1)}, u32[]{:S(2)}) copy-start(bf16[256,5120]{1,0:T(8,128)(2,1)} %text.2) | copy-start | bytes 7864324
  11.8 24.0 %collective-permute-start = (bf16[768,640]{1,0:T(8,128)(2,1)}, bf16[768,640]{1,0:T(8,128)(2,1)}, u32[]{:S(2)}, u32[]{:S(2)}) collective-permute-start(bf16[768,640]{1,0:T(8,128)(2,1)} %w0.1), channel_id=1, source_target_pairs={{0,32},{16,112},{32,0},{48,80},{64,96},{80,48},{96,64},{112,16},{1... | collective-permute-start | bytes 2949128 | tf_op jit(solution)/shard_map/ppermute | solution.py:454
  16.7 21.0 %collective-permute-start.2 = (bf16[768,640]{1,0:T(8,128)(2,1)}, bf16[768,640]{1,0:T(8,128)(2,1)}, u32[]{:S(2)}, u32[]{:S(2)}) collective-permute-start(bf16[768,640]{1,0:T(8,128)(2,1)} %collective-permute-done.1.w2), channel_id=1, source_target_pairs={{0,112},{16,32},{32,80},{48,0},{64,48},{80,96},{96,16},{112,64},{1... | collective-permute-start | bytes 2949128 | tf_op jit(solution)/shard_map/ppermute | solution.py:454
  16.7 19.1 %all-to-all-start = ((bf16[16,32,896]{2,1,0:T(8,128)(2,1)}), bf16[16,32,896]{2,1,0:T(8,128)(2,1)}, u32[]{:S(2)}, u32[]{:S(2)}) async-start(bf16[16,32,896]{2,1,0:T(8,128)(2,1)} %attend.1), calls=%async_computation | async-start | bytes 1835008 | tf_op jit(solution)/shard_map/all_to_all | solution.py:469
  24.4 16.8 %collective-permute-start.3 = (bf16[768,640]{1,0:T(8,128)(2,1)}, bf16[768,640]{1,0:T(8,128)(2,1)}, u32[]{:S(2)}, u32[]{:S(2)}) collective-permute-start(bf16[768,640]{1,0:T(8,128)(2,1)} %w0.1), channel_id=1, source_target_pairs={{0,16},{16,0},{32,48},{48,32},{64,80},{80,64},{96,112},{112,96},{1... | collective-permute-start | bytes 2949128 | tf_op jit(solution)/shard_map/ppermute | solution.py:454
  28.0 13.2 %collective-permute-start.4 = (bf16[768,640]{1,0:T(8,128)(2,1)}, bf16[768,640]{1,0:T(8,128)(2,1)}, u32[]{:S(2)}, u32[]{:S(2)}) collective-permute-start(bf16[768,640]{1,0:T(8,128)(2,1)} %collective-permute-done.1.w2), channel_id=1, source_target_pairs={{0,16},{16,0},{32,48},{48,32},{64,80},{80,64},{96,112},{112,96},{1... | collective-permute-start | bytes 2949128 | tf_op jit(solution)/shard_map/ppermute | solution.py:454
  37.7 9.9 %collective-permute-start.5 = (bf16[768,640]{1,0:T(8,128)(2,1)}, bf16[768,640]{1,0:T(8,128)(2,1)}, u32[]{:S(2)}, u32[]{:S(2)}) collective-permute-start(bf16[768,640]{1,0:T(8,128)(2,1)} %collective-permute-done.w4), channel_id=1, source_target_pairs={{0,16},{16,0},{32,48},{48,32},{64,80},{80,64},{96,112},{112,96},{1... | collective-permute-start | bytes 2949128 | tf_op jit(solution)/shard_map/ppermute | solution.py:454
  41.1 6.5 %collective-permute-start.6 = (bf16[768,640]{1,0:T(8,128)(2,1)}, bf16[768,640]{1,0:T(8,128)(2,1)}, u32[]{:S(2)}, u32[]{:S(2)}) collective-permute-start(bf16[768,640]{1,0:T(8,128)(2,1)} %collective-permute-done.2.w5), channel_id=1, source_target_pairs={{0,16},{16,0},{32,48},{48,32},{64,80},{80,64},{96,112},{112,96},{1... | collective-permute-start | bytes 2949128 | tf_op jit(solution)/shard_map/ppermute | solution.py:454

commit v3 on v2

--- a/solution.py
+++ b/solution.py
@@ -260,13 +260,15 @@
         pltpu.make_async_copy(source, weights.at[i], weight_sems.at[i])
         for i, source in enumerate((w0, w1, w2, w3, w4, w5))
     ]
-    for copy in loads + blocks:
+    for copy in loads:
         copy.start()
     loads[0].wait()
     begin, shift = window_of(starts)
     fetch = pltpu.make_async_copy(text.at[pl.ds(begin, WINDOW)], window, sems.at[7])
     fetch.start()
     loads[1].wait()
+    for copy in blocks:
+        copy.start()
     stat = parts[:, :, WIDTH:].astype(f32).reshape(COLUMNS * VQ, STATS)
 
     def shifted(n):

time: 52.2 us -> 51.4 us (0.985)
  Pallas kernels: 22.2 us -> 21.1 us
    pallas_call x1, Pallas kernels: 6.35 us -> 5.27 us  [merge(): pl.pallas_call(merge_kernel, out_shape=[jax.ShapeDtypeStruct((WINDOW, WID...]
  transfers between devices with their start and end apart: 8 -> 8, of which waited for: 3 -> 3; matrix products, arithmetic and copies ran while one was open for 2% -> 2% of each run, Pallas kernels for 35% -> 34%
where the time goes in v3:
time: 51.4 us; the launch traced here: 50.5 us
  Pallas kernels  21.1 us (41%)
  starting transfers between devices  19.6 us (38%)
  waiting for transfers between devices  8.47 us (16%)
  local copies, waits for them, and re-layouts  1.2 us (2%)
    ppermute x7, starting transfers between devices, move(): return lax.ppermute(x, 'tm', [(k, target(k)) for k in range(8)])  12 us
    pallas_call x1, Pallas kernels, attend(): pl.pallas_call(attend_kernel, out_shape=jax.ShapeDtypeStruct((COLUMNS, VQ...  9.05 us
    all_to_all x1, starting transfers between devices, per_device(): lax.all_to_all(parts, 'video', split_axis=0, concat_axis=0, tiled=True)  7.64 us
    pallas_call x1, Pallas kernels, merge(): pl.pallas_call(merge_kernel, out_shape=[jax.ShapeDtypeStruct((WINDOW, WID...  5.27 us
    ppermute x7, waiting for transfers between devices, move(): return lax.ppermute(x, 'tm', [(k, target(k)) for k in range(8)])  4.69 us
    pallas_call x1, Pallas kernels, place(): pl.pallas_call(place_kernel, out_shape=jax.ShapeDtypeStruct(normed.shape,...  3.99 us
    all_to_all x1, waiting for transfers between devices, per_device(): lax.all_to_all(parts, 'video', split_axis=0, concat_axis=0, tiled=True)  3.77 us
    pallas_call x1, Pallas kernels, norm_text(): pl.pallas_call(text_kernel, out_shape=jax.ShapeDtypeStruct(text.shape, bf...  2.8 us
  transfers between devices with their start and end apart: 8, of which 3 were waited for; matrix products, arithmetic and copies ran while one was open for 2% of the time, Pallas kernels for 34%

profile of v3, /device:TPU:1, one launch (start us, length us, event | category | flops | bytes accessed | tf_op | source)
XLA Modules:
  0.0 50.5 jit_solution(6991161638232046732)
XLA Ops:
  0.0 0.0 copy-start.2
  0.0 0.0 copy-start.3
  0.0 0.0 copy-start.1
  0.0 2.8 %collective-permute-start.1 = (bf16[768,640]{1,0:T(8,128)(2,1)}, bf16[768,640]{1,0:T(8,128)(2,1)}, u32[]{:S(2)}, u32[]{:S(2)}) collective-permute-start(bf16[768,640]{1,0:T(8,128)(2,1)} %w0.1), channel_id=1, source_target_pairs={{0,112},{16,32},{32,80},{48,0},{64,48},{80,96},{96,16},{112,64},{1... | collective-permute-start | bytes 2949128 | tf_op jit(solution)/shard_map/ppermute | solution.py:456
  2.8 0.0 copy-start
  2.8 9.1 %attend.1 = bf16[16,32,896]{2,1,0:T(8,128)(2,1)} custom-call(s32[16,64]{1,0:T(8,128)} %selected_in.1, s32[16]{0:T(128)} %counts_in.1, s32[128]{0:T(128)} %starts_in.5, bf16[16,8,32,768]{3,2,1,0:T(8,128)(2,1)} %frames.1, bf16[64,768]{1,0:T(8,128)(2,1)} %pos_in.1, bf16[32,768]{1,0:T(8,128)(2,1)} %queries_in.3, bf16[768,768]{1,0:T(8,128)(2,1)} %w_query_in.1, ...), custom_call_target="tpu_custom_call" | custom-call | flops 8999999488 | bytes 8000000 | tf_op jit(solution)/shard_map/attend/pallas_call | solution.py:186
  11.8 2.1 %collective-permute-start = (bf16[768,640]{1,0:T(8,128)(2,1)}, bf16[768,640]{1,0:T(8,128)(2,1)}, u32[]{:S(2)}, u32[]{:S(2)}) collective-permute-start(bf16[768,640]{1,0:T(8,128)(2,1)} %w0.1), channel_id=1, source_target_pairs={{0,32},{16,112},{32,0},{48,80},{64,96},{80,48},{96,64},{112,16},{1... | collective-permute-start | bytes 2949128 | tf_op jit(solution)/shard_map/ppermute | solution.py:456
  13.9 2.8 %collective-permute-done.1.w2 = bf16[768,640]{1,0:T(8,128)(2,1)} collective-permute-done((bf16[768,640]{1,0:T(8,128)(2,1)}, bf16[768,640]{1,0:T(8,128)(2,1)}, u32[]{:S(2)}, u32[]{:S(2)}) %collective-permute-start.1) | collective-permute-done | bytes 983072 | tf_op jit(solution)/shard_map/ppermute | solution.py:456
  16.7 0.0 collective-permute-start.2
  16.7 7.6 %all-to-all-start = ((bf16[16,32,896]{2,1,0:T(8,128)(2,1)}), bf16[16,32,896]{2,1,0:T(8,128)(2,1)}, u32[]{:S(2)}, u32[]{:S(2)}) async-start(bf16[16,32,896]{2,1,0:T(8,128)(2,1)} %attend.1), calls=%async_computation | async-start | bytes 1835008 | tf_op jit(solution)/shard_map/all_to_all | solution.py:471
  24.3 3.6 %collective-permute-start.3 = (bf16[768,640]{1,0:T(8,128)(2,1)}, bf16[768,640]{1,0:T(8,128)(2,1)}, u32[]{:S(2)}, u32[]{:S(2)}) collective-permute-start(bf16[768,640]{1,0:T(8,128)(2,1)} %w0.1), channel_id=1, source_target_pairs={{0,16},{16,0},{32,48},{48,32},{64,80},{80,64},{96,112},{112,96},{1... | collective-permute-start | bytes 2949128 | tf_op jit(solution)/shard_map/ppermute | solution.py:456
  27.9 0.1 collective-permute-start.4
  28.0 0.0 copy-done.2
  28.0 0.6 %reshape.13.gain_in = f32[1,768]{1,0:T(1,128)} reshape(f32[768]{0:T(1024)S(1)} %copy-done.2) | data formatting | bytes 6144 | tf_op jit(solution)/shard_map/reshape | solution.py:473
  28.6 0.0 copy-done.3
  28.6 0.6 %reshape.14.bias_in = f32[1,768]{1,0:T(1,128)} reshape(f32[768]{0:T(1024)S(1)} %copy-done.3) | data formatting | bytes 6144 | tf_op jit(solution)/shard_map/reshape | solution.py:473
  29.2 0.0 copy-done.1
  29.2 0.0 copy-done
  29.2 2.8 %norm_text.1.normed = bf16[256,5120]{1,0:T(8,128)(2,1)} custom-call(bf16[256,5120]{1,0:T(8,128)(2,1)S(1)} %copy-done, f32[1,5120]{1,0:T(1,128)S(1)} %bitcast.3), custom_call_target="tpu_custom_call" | custom-call | flops 8000000 | bytes 5300000 | tf_op jit(solution)/shard_map/norm_text/pallas_call | solution.py:436
  32.0 3.8 %all-to-all-done.parts_in = bf16[16,32,896]{2,1,0:T(8,128)(2,1)} async-done(((bf16[16,32,896]{2,1,0:T(8,128)(2,1)}), bf16[16,32,896]{2,1,0:T(8,128)(2,1)}, u32[]{:S(2)}, u32[]{:S(2)}) %all-to-all-start) | async-done | bytes 917536 | tf_op jit(solution)/shard_map/all_to_all | solution.py:471
  35.8 0.0 collective-permute-done.w4
  35.8 1.9 %collective-permute-done.2.w5 = bf16[768,640]{1,0:T(8,128)(2,1)} collective-permute-done((bf16[768,640]{1,0:T(8,128)(2,1)}, bf16[768,640]{1,0:T(8,128)(2,1)}, u32[]{:S(2)}, u32[]{:S(2)}) %collective-permute-start.2) | collective-permute-done | bytes 983072 | tf_op jit(solution)/shard_map/ppermute | solution.py:456
  37.7 3.4 %collective-permute-start.5 = (bf16[768,640]{1,0:T(8,128)(2,1)}, bf16[768,640]{1,0:T(8,128)(2,1)}, u32[]{:S(2)}, u32[]{:S(2)}) collective-permute-start(bf16[768,640]{1,0:T(8,128)(2,1)} %collective-permute-done.w4), channel_id=1, source_target_pairs={{0,16},{16,0},{32,48},{48,32},{64,80},{80,64},{96,112},{112,96},{1... | collective-permute-start | bytes 2949128 | tf_op jit(solution)/shard_map/ppermute | solution.py:456
  41.1 0.1 collective-permute-start.6
  41.2 0.0 collective-permute-done.3.w1
  41.2 0.0 collective-permute-done.4.w3
  41.2 5.3 %merge.1 = (bf16[48,768]{1,0:T(8,128)(2,1)}, bf16[48,3840]{1,0:T(8,128)(2,1)}, bf16[48,1280]{1,0:T(8,128)(2,1)}) custom-call(bf16[16,32,896]{2,1,0:T(8,128)(2,1)} %all-to-all-done.parts_in, bf16[32,768]{1,0:T(8,128)(2,1)} %queries_in.3, bf16[768,768]{1,0:T(8,128)(2,1)} %w_out_in.1, f32[1,768]{1,0:T(1,128)} %reshape.13.gain_in, f32[1,768]{1,0:T(1,128)} %reshape.14.bias_in, ...), custom_call_target="tpu_custom_call" | custom-call | flops 500000000 | bytes 9000000 | tf_op jit(solution)/shard_map/merge/pallas_call | solution.py:328
  46.5 0.0 collective-permute-done.5.w6
  46.5 0.0 collective-permute-done.6.w7
  46.5 4.0 %place.1 = bf16[256,5120]{1,0:T(8,128)(2,1)} custom-call(bf16[48,768]{1,0:T(8,128)(2,1)} %get-tuple-element.35.rows_in, bf16[48,3840]{1,0:T(8,128)(2,1)} %get-tuple-element.36.wide_in, bf16[48,1280]{1,0:T(8,128)(2,1)} %get-tuple-element.37.rest_in, s32[128]{0:T(128)} %starts_in.5, f32[1,5120]{1,0:T(1,128)} %bitcast.5, ...), custom_call_target="tpu_custom_call", output_to_operand_aliasing={{}: (6, {})} | custom-call | tf_op jit(solution)/shard_map/place/pallas_call | solution.py:404
Async XLA Ops:
  0.0 28.0 %copy-start.2 = (f32[768]{0:T(1024)S(1)}, f32[768]{0:T(1024)}, u32[]{:S(2)}) copy-start(f32[768]{0:T(1024)} %param.26) | copy-start | bytes 9220
  0.0 28.6 %copy-start.3 = (f32[768]{0:T(1024)S(1)}, f32[768]{0:T(1024)}, u32[]{:S(2)}) copy-start(f32[768]{0:T(1024)} %param.27) | copy-start | bytes 9220
  0.0 29.2 %copy-start.1 = (f32[5120]{0:T(1024)S(1)}, f32[5120]{0:T(1024)}, u32[]{:S(2)}) copy-start(f32[5120]{0:T(1024)} %param.31) | copy-start | bytes 61444
  0.0 16.7 %collective-permute-start.1 = (bf16[768,640]{1,0:T(8,128)(2,1)}, bf16[768,640]{1,0:T(8,128)(2,1)}, u32[]{:S(2)}, u32[]{:S(2)}) collective-permute-start(bf16[768,640]{1,0:T(8,128)(2,1)} %w0.1), channel_id=1, source_target_pairs={{0,112},{16,32},{32,80},{48,0},{64,48},{80,96},{96,16},{112,64},{1... | collective-permute-start | bytes 2949128 | tf_op jit(solution)/shard_map/ppermute | solution.py:456
  2.8 26.5 %copy-start = (bf16[256,5120]{1,0:T(8,128)(2,1)S(1)}, bf16[256,5120]{1,0:T(8,128)(2,1)}, u32[]{:S(2)}) copy-start(bf16[256,5120]{1,0:T(8,128)(2,1)} %text.2) | copy-start | bytes 7864324
  11.8 24.0 %collective-permute-start = (bf16[768,640]{1,0:T(8,128)(2,1)}, bf16[768,640]{1,0:T(8,128)(2,1)}, u32[]{:S(2)}, u32[]{:S(2)}) collective-permute-start(bf16[768,640]{1,0:T(8,128)(2,1)} %w0.1), channel_id=1, source_target_pairs={{0,32},{16,112},{32,0},{48,80},{64,96},{80,48},{96,64},{112,16},{1... | collective-permute-start | bytes 2949128 | tf_op jit(solution)/shard_map/ppermute | solution.py:456
  16.7 21.0 %collective-permute-start.2 = (bf16[768,640]{1,0:T(8,128)(2,1)}, bf16[768,640]{1,0:T(8,128)(2,1)}, u32[]{:S(2)}, u32[]{:S(2)}) collective-permute-start(bf16[768,640]{1,0:T(8,128)(2,1)} %collective-permute-done.1.w2), channel_id=1, source_target_pairs={{0,112},{16,32},{32,80},{48,0},{64,48},{80,96},{96,16},{112,64},{1... | collective-permute-start | bytes 2949128 | tf_op jit(solution)/shard_map/ppermute | solution.py:456
  16.7 19.1 %all-to-all-start = ((bf16[16,32,896]{2,1,0:T(8,128)(2,1)}), bf16[16,32,896]{2,1,0:T(8,128)(2,1)}, u32[]{:S(2)}, u32[]{:S(2)}) async-start(bf16[16,32,896]{2,1,0:T(8,128)(2,1)} %attend.1), calls=%async_computation | async-start | bytes 1835008 | tf_op jit(solution)/shard_map/all_to_all | solution.py:471
  24.3 16.8 %collective-permute-start.3 = (bf16[768,640]{1,0:T(8,128)(2,1)}, bf16[768,640]{1,0:T(8,128)(2,1)}, u32[]{:S(2)}, u32[]{:S(2)}) collective-permute-start(bf16[768,640]{1,0:T(8,128)(2,1)} %w0.1), channel_id=1, source_target_pairs={{0,16},{16,0},{32,48},{48,32},{64,80},{80,64},{96,112},{112,96},{1... | collective-permute-start | bytes 2949128 | tf_op jit(solution)/shard_map/ppermute | solution.py:456
  27.9 13.2 %collective-permute-start.4 = (bf16[768,640]{1,0:T(8,128)(2,1)}, bf16[768,640]{1,0:T(8,128)(2,1)}, u32[]{:S(2)}, u32[]{:S(2)}) collective-permute-start(bf16[768,640]{1,0:T(8,128)(2,1)} %collective-permute-done.1.w2), channel_id=1, source_target_pairs={{0,16},{16,0},{32,48},{48,32},{64,80},{80,64},{96,112},{112,96},{1... | collective-permute-start | bytes 2949128 | tf_op jit(solution)/shard_map/ppermute | solution.py:456
  37.7 8.8 %collective-permute-start.5 = (bf16[768,640]{1,0:T(8,128)(2,1)}, bf16[768,640]{1,0:T(8,128)(2,1)}, u32[]{:S(2)}, u32[]{:S(2)}) collective-permute-start(bf16[768,640]{1,0:T(8,128)(2,1)} %collective-permute-done.w4), channel_id=1, source_target_pairs={{0,16},{16,0},{32,48},{48,32},{64,80},{80,64},{96,112},{112,96},{1... | collective-permute-start | bytes 2949128 | tf_op jit(solution)/shard_map/ppermute | solution.py:456
  41.1 5.4 %collective-permute-start.6 = (bf16[768,640]{1,0:T(8,128)(2,1)}, bf16[768,640]{1,0:T(8,128)(2,1)}, u32[]{:S(2)}, u32[]{:S(2)}) collective-permute-start(bf16[768,640]{1,0:T(8,128)(2,1)} %collective-permute-done.2.w5), channel_id=1, source_target_pairs={{0,16},{16,0},{32,48},{48,32},{64,80},{80,64},{96,112},{112,96},{1... | collective-permute-start | bytes 2949128 | tf_op jit(solution)/shard_map/ppermute | solution.py:456

commit v4 on v3

--- a/solution.py
+++ b/solution.py
@@ -390,12 +390,17 @@
         squares = squares + jnp.sum(embeds * embeds, axis=-1, keepdims=True)
     scale = lax.rsqrt(squares * (1.0 / DL) + 1e-05)
     loads[2].wait()
+    stores = []
     for i, block in enumerate(all_blocks):
         here = pl.ds(pl.multiple_of(block * SHARE, 128), SHARE)
         done_rows[:, here] = (wide[:, i * SHARE:(i + 1) * SHARE] * scale * norm_gain[:, here]).astype(bf16)
-    store = pltpu.make_async_copy(done_rows, done.at[pl.ds(begin, WINDOW)], sems.at[3])
-    store.start()
-    store.wait()
+        store = pltpu.make_async_copy(
+            done_rows.at[:, here], done.at[pl.ds(begin, WINDOW), here], sems.at[3 + i]
+        )
+        store.start()
+        stores.append(store)
+    for store in stores:
+        store.wait()
 
 
 def place(rows, wide, rest, starts, proj_bias, norm_gain, normed, weights):
@@ -414,7 +419,7 @@
             pltpu.VMEM((8 - NEAR, WIDTH, SHARE), bf16),
             pltpu.VMEM((WINDOW, DL), f32),
             pltpu.VMEM((WINDOW, DL), bf16),
-            pltpu.SemaphoreType.DMA((4,)),
+            pltpu.SemaphoreType.DMA((11,)),
             pltpu.SemaphoreType.DMA((8 - NEAR,)),
         ],
         compiler_params=pltpu.CompilerParams(vmem_limit_bytes=MERGE_VMEM),

time: 51.4 us -> 51.4 us (level)
  no operation moved by 1% of the time
where the time goes in v4:
time: 51.4 us; the launch traced here: 50.5 us
  Pallas kernels  21.1 us (41%)
  starting transfers between devices  19.6 us (38%)
  waiting for transfers between devices  8.51 us (17%)
  local copies, waits for them, and re-layouts  1.2 us (2%)
    ppermute x7, starting transfers between devices, move(): return lax.ppermute(x, 'tm', [(k, target(k)) for k in range(8)])  12 us
    pallas_call x1, Pallas kernels, attend(): pl.pallas_call(attend_kernel, out_shape=jax.ShapeDtypeStruct((COLUMNS, VQ...  9.04 us
    all_to_all x1, starting transfers between devices, per_device(): lax.all_to_all(parts, 'video', split_axis=0, concat_axis=0, tiled=True)  7.64 us
    pallas_call x1, Pallas kernels, merge(): pl.pallas_call(merge_kernel, out_shape=[jax.ShapeDtypeStruct((WINDOW, WID...  5.28 us
    ppermute x7, waiting for transfers between devices, move(): return lax.ppermute(x, 'tm', [(k, target(k)) for k in range(8)])  4.76 us
    pallas_call x1, Pallas kernels, place(): pl.pallas_call(place_kernel, out_shape=jax.ShapeDtypeStruct(normed.shape,...  4 us
    all_to_all x1, waiting for transfers between devices, per_device(): lax.all_to_all(parts, 'video', split_axis=0, concat_axis=0, tiled=True)  3.76 us
    pallas_call x1, Pallas kernels, norm_text(): pl.pallas_call(text_kernel, out_shape=jax.ShapeDtypeStruct(text.shape, bf...  2.8 us
  transfers between devices with their start and end apart: 8, of which 3 were waited for; matrix products, arithmetic and copies ran while one was open for 2% of the time, Pallas kernels for 34%

profile of v4, /device:TPU:1, one launch (start us, length us, event | category | flops | bytes accessed | tf_op | source)
XLA Modules:
  0.0 50.5 jit_solution(15243345815990994410)
XLA Ops:
  0.0 0.0 copy-start.2
  0.0 0.0 copy-start.3
  0.0 0.0 copy-start.1
  0.0 2.8 %collective-permute-start.1 = (bf16[768,640]{1,0:T(8,128)(2,1)}, bf16[768,640]{1,0:T(8,128)(2,1)}, u32[]{:S(2)}, u32[]{:S(2)}) collective-permute-start(bf16[768,640]{1,0:T(8,128)(2,1)} %w0.1), channel_id=1, source_target_pairs={{0,112},{16,32},{32,80},{48,0},{64,48},{80,96},{96,16},{112,64},{1... | collective-permute-start | bytes 2949128 | tf_op jit(solution)/shard_map/ppermute | solution.py:461
  2.8 0.0 copy-start
  2.8 9.0 %attend.1 = bf16[16,32,896]{2,1,0:T(8,128)(2,1)} custom-call(s32[16,64]{1,0:T(8,128)} %selected_in.1, s32[16]{0:T(128)} %counts_in.1, s32[128]{0:T(128)} %starts_in.5, bf16[16,8,32,768]{3,2,1,0:T(8,128)(2,1)} %frames.1, bf16[64,768]{1,0:T(8,128)(2,1)} %pos_in.1, bf16[32,768]{1,0:T(8,128)(2,1)} %queries_in.3, bf16[768,768]{1,0:T(8,128)(2,1)} %w_query_in.1, ...), custom_call_target="tpu_custom_call" | custom-call | flops 8999999488 | bytes 8000000 | tf_op jit(solution)/shard_map/attend/pallas_call | solution.py:186
  11.8 2.0 %collective-permute-start = (bf16[768,640]{1,0:T(8,128)(2,1)}, bf16[768,640]{1,0:T(8,128)(2,1)}, u32[]{:S(2)}, u32[]{:S(2)}) collective-permute-start(bf16[768,640]{1,0:T(8,128)(2,1)} %w0.1), channel_id=1, source_target_pairs={{0,32},{16,112},{32,0},{48,80},{64,96},{80,48},{96,64},{112,16},{1... | collective-permute-start | bytes 2949128 | tf_op jit(solution)/shard_map/ppermute | solution.py:461
  13.8 2.9 %collective-permute-done.1.w2 = bf16[768,640]{1,0:T(8,128)(2,1)} collective-permute-done((bf16[768,640]{1,0:T(8,128)(2,1)}, bf16[768,640]{1,0:T(8,128)(2,1)}, u32[]{:S(2)}, u32[]{:S(2)}) %collective-permute-start.1) | collective-permute-done | bytes 983072 | tf_op jit(solution)/shard_map/ppermute | solution.py:461
  16.7 0.0 collective-permute-start.2
  16.7 7.6 %all-to-all-start = ((bf16[16,32,896]{2,1,0:T(8,128)(2,1)}), bf16[16,32,896]{2,1,0:T(8,128)(2,1)}, u32[]{:S(2)}, u32[]{:S(2)}) async-start(bf16[16,32,896]{2,1,0:T(8,128)(2,1)} %attend.1), calls=%async_computation | async-start | bytes 1835008 | tf_op jit(solution)/shard_map/all_to_all | solution.py:476
  24.4 3.6 %collective-permute-start.3 = (bf16[768,640]{1,0:T(8,128)(2,1)}, bf16[768,640]{1,0:T(8,128)(2,1)}, u32[]{:S(2)}, u32[]{:S(2)}) collective-permute-start(bf16[768,640]{1,0:T(8,128)(2,1)} %w0.1), channel_id=1, source_target_pairs={{0,16},{16,0},{32,48},{48,32},{64,80},{80,64},{96,112},{112,96},{1... | collective-permute-start | bytes 2949128 | tf_op jit(solution)/shard_map/ppermute | solution.py:461
  28.0 0.1 collective-permute-start.4
  28.0 0.0 copy-done.2
  28.1 0.6 %reshape.13.gain_in = f32[1,768]{1,0:T(1,128)} reshape(f32[768]{0:T(1024)S(1)} %copy-done.2) | data formatting | bytes 6144 | tf_op jit(solution)/shard_map/reshape | solution.py:478
  28.6 0.0 copy-done.3
  28.6 0.6 %reshape.14.bias_in = f32[1,768]{1,0:T(1,128)} reshape(f32[768]{0:T(1024)S(1)} %copy-done.3) | data formatting | bytes 6144 | tf_op jit(solution)/shard_map/reshape | solution.py:478
  29.2 0.0 copy-done.1
  29.2 0.0 copy-done
  29.2 2.8 %norm_text.1.normed = bf16[256,5120]{1,0:T(8,128)(2,1)} custom-call(bf16[256,5120]{1,0:T(8,128)(2,1)S(1)} %copy-done, f32[1,5120]{1,0:T(1,128)S(1)} %bitcast.3), custom_call_target="tpu_custom_call" | custom-call | flops 8000000 | bytes 5300000 | tf_op jit(solution)/shard_map/norm_text/pallas_call | solution.py:441
  32.0 3.8 %all-to-all-done.parts_in = bf16[16,32,896]{2,1,0:T(8,128)(2,1)} async-done(((bf16[16,32,896]{2,1,0:T(8,128)(2,1)}), bf16[16,32,896]{2,1,0:T(8,128)(2,1)}, u32[]{:S(2)}, u32[]{:S(2)}) %all-to-all-start) | async-done | bytes 917536 | tf_op jit(solution)/shard_map/all_to_all | solution.py:476
  35.8 0.0 collective-permute-done.w4
  35.8 1.9 %collective-permute-done.2.w5 = bf16[768,640]{1,0:T(8,128)(2,1)} collective-permute-done((bf16[768,640]{1,0:T(8,128)(2,1)}, bf16[768,640]{1,0:T(8,128)(2,1)}, u32[]{:S(2)}, u32[]{:S(2)}) %collective-permute-start.2) | collective-permute-done | bytes 983072 | tf_op jit(solution)/shard_map/ppermute | solution.py:461
  37.7 3.4 %collective-permute-start.5 = (bf16[768,640]{1,0:T(8,128)(2,1)}, bf16[768,640]{1,0:T(8,128)(2,1)}, u32[]{:S(2)}, u32[]{:S(2)}) collective-permute-start(bf16[768,640]{1,0:T(8,128)(2,1)} %collective-permute-done.w4), channel_id=1, source_target_pairs={{0,16},{16,0},{32,48},{48,32},{64,80},{80,64},{96,112},{112,96},{1... | collective-permute-start | bytes 2949128 | tf_op jit(solution)/shard_map/ppermute | solution.py:461
  41.1 0.1 collective-permute-start.6
  41.2 0.0 collective-permute-done.3.w1
  41.2 0.0 collective-permute-done.4.w3
  41.2 5.3 %merge.1 = (bf16[48,768]{1,0:T(8,128)(2,1)}, bf16[48,3840]{1,0:T(8,128)(2,1)}, bf16[48,1280]{1,0:T(8,128)(2,1)}) custom-call(bf16[16,32,896]{2,1,0:T(8,128)(2,1)} %all-to-all-done.parts_in, bf16[32,768]{1,0:T(8,128)(2,1)} %queries_in.3, bf16[768,768]{1,0:T(8,128)(2,1)} %w_out_in.1, f32[1,768]{1,0:T(1,128)} %reshape.13.gain_in, f32[1,768]{1,0:T(1,128)} %reshape.14.bias_in, ...), custom_call_target="tpu_custom_call" | custom-call | flops 500000000 | bytes 9000000 | tf_op jit(solution)/shard_map/merge/pallas_call | solution.py:328
  46.5 0.0 collective-permute-done.5.w6
  46.5 0.0 collective-permute-done.6.w7
  46.5 4.0 %place.1 = bf16[256,5120]{1,0:T(8,128)(2,1)} custom-call(bf16[48,768]{1,0:T(8,128)(2,1)} %get-tuple-element.35.rows_in, bf16[48,3840]{1,0:T(8,128)(2,1)} %get-tuple-element.36.wide_in, bf16[48,1280]{1,0:T(8,128)(2,1)} %get-tuple-element.37.rest_in, s32[128]{0:T(128)} %starts_in.5, f32[1,5120]{1,0:T(1,128)} %bitcast.5, ...), custom_call_target="tpu_custom_call", output_to_operand_aliasing={{}: (6, {})} | custom-call | tf_op jit(solution)/shard_map/place/pallas_call | solution.py:409
Async XLA Ops:
  0.0 28.1 %copy-start.2 = (f32[768]{0:T(1024)S(1)}, f32[768]{0:T(1024)}, u32[]{:S(2)}) copy-start(f32[768]{0:T(1024)} %param.26) | copy-start | bytes 9220
  0.0 28.6 %copy-start.3 = (f32[768]{0:T(1024)S(1)}, f32[768]{0:T(1024)}, u32[]{:S(2)}) copy-start(f32[768]{0:T(1024)} %param.27) | copy-start | bytes 9220
  0.0 29.2 %copy-start.1 = (f32[5120]{0:T(1024)S(1)}, f32[5120]{0:T(1024)}, u32[]{:S(2)}) copy-start(f32[5120]{0:T(1024)} %param.31) | copy-start | bytes 61444
  0.0 16.7 %collective-permute-start.1 = (bf16[768,640]{1,0:T(8,128)(2,1)}, bf16[768,640]{1,0:T(8,128)(2,1)}, u32[]{:S(2)}, u32[]{:S(2)}) collective-permute-start(bf16[768,640]{1,0:T(8,128)(2,1)} %w0.1), channel_id=1, source_target_pairs={{0,112},{16,32},{32,80},{48,0},{64,48},{80,96},{96,16},{112,64},{1... | collective-permute-start | bytes 2949128 | tf_op jit(solution)/shard_map/ppermute | solution.py:461
  2.8 26.5 %copy-start = (bf16[256,5120]{1,0:T(8,128)(2,1)S(1)}, bf16[256,5120]{1,0:T(8,128)(2,1)}, u32[]{:S(2)}) copy-start(bf16[256,5120]{1,0:T(8,128)(2,1)} %text.2) | copy-start | bytes 7864324
  11.8 24.0 %collective-permute-start = (bf16[768,640]{1,0:T(8,128)(2,1)}, bf16[768,640]{1,0:T(8,128)(2,1)}, u32[]{:S(2)}, u32[]{:S(2)}) collective-permute-start(bf16[768,640]{1,0:T(8,128)(2,1)} %w0.1), channel_id=1, source_target_pairs={{0,32},{16,112},{32,0},{48,80},{64,96},{80,48},{96,64},{112,16},{1... | collective-permute-start | bytes 2949128 | tf_op jit(solution)/shard_map/ppermute | solution.py:461
  16.7 21.0 %collective-permute-start.2 = (bf16[768,640]{1,0:T(8,128)(2,1)}, bf16[768,640]{1,0:T(8,128)(2,1)}, u32[]{:S(2)}, u32[]{:S(2)}) collective-permute-start(bf16[768,640]{1,0:T(8,128)(2,1)} %collective-permute-done.1.w2), channel_id=1, source_target_pairs={{0,112},{16,32},{32,80},{48,0},{64,48},{80,96},{96,16},{112,64},{1... | collective-permute-start | bytes 2949128 | tf_op jit(solution)/shard_map/ppermute | solution.py:461
  16.7 19.1 %all-to-all-start = ((bf16[16,32,896]{2,1,0:T(8,128)(2,1)}), bf16[16,32,896]{2,1,0:T(8,128)(2,1)}, u32[]{:S(2)}, u32[]{:S(2)}) async-start(bf16[16,32,896]{2,1,0:T(8,128)(2,1)} %attend.1), calls=%async_computation | async-start | bytes 1835008 | tf_op jit(solution)/shard_map/all_to_all | solution.py:476
  24.4 16.8 %collective-permute-start.3 = (bf16[768,640]{1,0:T(8,128)(2,1)}, bf16[768,640]{1,0:T(8,128)(2,1)}, u32[]{:S(2)}, u32[]{:S(2)}) collective-permute-start(bf16[768,640]{1,0:T(8,128)(2,1)} %w0.1), channel_id=1, source_target_pairs={{0,16},{16,0},{32,48},{48,32},{64,80},{80,64},{96,112},{112,96},{1... | collective-permute-start | bytes 2949128 | tf_op jit(solution)/shard_map/ppermute | solution.py:461
  28.0 13.2 %collective-permute-start.4 = (bf16[768,640]{1,0:T(8,128)(2,1)}, bf16[768,640]{1,0:T(8,128)(2,1)}, u32[]{:S(2)}, u32[]{:S(2)}) collective-permute-start(bf16[768,640]{1,0:T(8,128)(2,1)} %collective-permute-done.1.w2), channel_id=1, source_target_pairs={{0,16},{16,0},{32,48},{48,32},{64,80},{80,64},{96,112},{112,96},{1... | collective-permute-start | bytes 2949128 | tf_op jit(solution)/shard_map/ppermute | solution.py:461
  37.7 8.8 %collective-permute-start.5 = (bf16[768,640]{1,0:T(8,128)(2,1)}, bf16[768,640]{1,0:T(8,128)(2,1)}, u32[]{:S(2)}, u32[]{:S(2)}) collective-permute-start(bf16[768,640]{1,0:T(8,128)(2,1)} %collective-permute-done.w4), channel_id=1, source_target_pairs={{0,16},{16,0},{32,48},{48,32},{64,80},{80,64},{96,112},{112,96},{1... | collective-permute-start | bytes 2949128 | tf_op jit(solution)/shard_map/ppermute | solution.py:461
  41.1 5.4 %collective-permute-start.6 = (bf16[768,640]{1,0:T(8,128)(2,1)}, bf16[768,640]{1,0:T(8,128)(2,1)}, u32[]{:S(2)}, u32[]{:S(2)}) collective-permute-start(bf16[768,640]{1,0:T(8,128)(2,1)} %collective-permute-done.2.w5), channel_id=1, source_target_pairs={{0,16},{16,0},{32,48},{48,32},{64,80},{80,64},{96,112},{112,96},{1... | collective-permute-start | bytes 2949128 | tf_op jit(solution)/shard_map/ppermute | solution.py:461
